TPU v7x, 32 devices: a whole 2x2x4 slice. The times are simulated.
32 devices in a mesh: depth: 16 (over z, y, x), rays: 2 (over core).
Axes of the slice: x: 2, y: 2, z: 4, core: 2. Of those that a mesh axis runs over, the one named last changes fastest.
Arguments:
- encoded: bfloat16 [16, 4, 1024, 256], P('depth', None, 'rays'), may hold values from -6 to 6
- deltas: float32 [16, 4, 1024], P('depth', None, 'rays'), may hold values from 0.015625 to 0.125
- w_in: bfloat16 [16, 256, 512], P('depth'), may hold values from -0.375 to 0.375
- w_mid: bfloat16 [16, 512, 512], P('depth'), may hold values from -0.25 to 0.25
- w_sigma: bfloat16 [16, 512], P('depth'), may hold values from -0.25 to 0.25
- order: int32 [2, 16], P('rays'), may hold values from 0 to 15, each once within a row
- target: bfloat16 [1024, 512], P('rays'), may hold values from -3 to 3
Outputs:
- grad_in: float32 [16, 256, 512], P('depth', 'rays')
- grad_mid: float32 [16, 512, 512], P('depth', 'rays')
- grad_sigma: float32 [16, 512], P('depth', 'rays')
- loss: float32 [], replicated
Inputs may be any that keep to these rules, and one draw needn't show every extreme that they name: Each row of order lists every region once.
All inputs are finite; a program needn't handle non-finite values.
Results may differ from a plain program's by a relative error of at most 0.015.
Values may be sent and summed in bfloat16 or wider, within the bound.
No kernel may reach another device: no remote copies, remote signals or barrier semaphores. Data moves between devices by JAX's collectives and lax.ppermute only.
A program may use at most 64 MiB of HBM per device.

v0:
```python
import jax
import jax.numpy as jnp
from jax import lax
from jax.sharding import PartitionSpec as P


def contract_rows(left, right):
    return lax.dot_general(
        left, right, (((0,), (0,)), ((), ())), preferred_element_type=jnp.float32
    )


def body(encoded, deltas, w_in, w_mid, w_sigma, order, target):
    samples = encoded.shape[1]
    rays_dev = encoded.shape[2]
    width_in = encoded.shape[3]
    rows = encoded[0].reshape(samples * rays_dev, width_in)
    first = w_in[0]
    second = w_mid[0]
    density = w_sigma[0]
    spacing = deltas[0]
    hidden = jnp.maximum(jnp.dot(rows, first, preferred_element_type=jnp.float32), 0.0)
    hidden_b = hidden.astype(jnp.bfloat16)
    feat = jnp.dot(hidden_b, second, preferred_element_type=jnp.float32)
    logit = jnp.dot(hidden_b, density, preferred_element_type=jnp.float32)
    features = feat.shape[1]
    tau = jax.nn.softplus(logit).reshape(samples, rays_dev) * spacing
    excl = jnp.cumsum(tau, axis=0) - tau
    weight = jnp.exp(-excl) * (1.0 - jnp.exp(-tau))
    feat3 = feat.reshape(samples, rays_dev, features)
    segment = jnp.sum(weight[:, :, None] * feat3, axis=0)
    depth_tau = jnp.sum(tau, axis=0)
    regions = lax.axis_size("depth")
    region_me = lax.axis_index("depth")
    positions = jnp.arange(regions, dtype=jnp.int32)
    onehot = order[0][:, None] == positions[None, :]
    rank = jnp.sum(jnp.where(onehot, positions[:, None], 0), axis=0)
    rank_me = jnp.sum(jnp.where(positions == region_me, rank, 0))
    before = (rank < rank_me).astype(jnp.float32)
    after = (rank > rank_me).astype(jnp.float32)
    all_tau = lax.all_gather(depth_tau[None], "depth", axis=0, tiled=True)
    prefix = jnp.dot(before, all_tau, precision=lax.Precision.HIGHEST)
    trans = jnp.exp(-prefix)
    weighted = trans[:, None] * segment
    count_total = rays_dev * lax.axis_size("rays") * features
    color = lax.psum(weighted, "depth")
    err = color - target.astype(jnp.float32)
    loss = lax.psum(jnp.sum(err * err), "rays") / count_total
    dcolor = lax.optimization_barrier(err.astype(jnp.bfloat16)).astype(jnp.float32)
    qsum = jnp.sum(segment * dcolor, axis=1)
    all_terms = lax.all_gather((trans * qsum)[None], "depth", axis=0, tiled=True)
    gtau = -jnp.dot(after, all_terms, precision=lax.Precision.HIGHEST)
    dseg = trans[:, None] * dcolor
    dfeat = (weight[:, :, None] * dseg[None]).astype(jnp.bfloat16)
    vsum = jnp.sum(feat3 * dseg[None], axis=2)
    wv = weight * vsum
    dtau = (
        jnp.exp(-(excl + tau)) * vsum
        - (jnp.sum(wv, axis=0)[None] - jnp.cumsum(wv, axis=0))
        + gtau[None]
    )
    dz = (dtau * spacing).reshape(-1) * jax.nn.sigmoid(logit)
    dfeat2 = dfeat.reshape(samples * rays_dev, features)
    part_mid = contract_rows(hidden_b, dfeat2)
    part_sig = jnp.sum(hidden_b * dz[:, None], axis=0)
    dhb = lax.dot_general(
        dfeat2, second, (((1,), (1,)), ((), ())), preferred_element_type=jnp.float32
    )
    dhb = dhb + dz[:, None] * density.astype(jnp.float32)[None]
    dpre = jnp.where(hidden > 0, dhb, 0.0).astype(jnp.bfloat16)
    part_in = contract_rows(rows, dpre)
    grad_in, grad_mid, grad_sigma = (
        lax.psum_scatter(
            part_in.astype(jnp.bfloat16), "rays", scatter_dimension=0, tiled=True
        ).astype(jnp.float32),
        lax.psum_scatter(
            part_mid.astype(jnp.bfloat16), "rays", scatter_dimension=0, tiled=True
        ).astype(jnp.float32),
        lax.psum_scatter(
            part_sig.astype(jnp.bfloat16), "rays", scatter_dimension=0, tiled=True
        ).astype(jnp.float32),
    )
    return (grad_in[None], grad_mid[None], grad_sigma[None], loss)


def solution(mesh):
    in_specs = (
        P("depth", None, "rays", None),
        P("depth", None, "rays"),
        P("depth", None, None),
        P("depth", None, None),
        P("depth", None),
        P("rays", None),
        P("rays", None),
    )
    out_specs = (P("depth", "rays", None), P("depth", "rays", None), P("depth", "rays"), P())
    return jax.shard_map(body, mesh=mesh, in_specs=in_specs, out_specs=out_specs, check_vma=False)
```

profile of v0, /device:TPU:0, one launch (start us, length us, event | category | flops | bytes accessed | tf_op | source)
XLA Modules:
  0.0 254.2 jit_solution(5504395839488759128)
XLA Ops:
  7.2 1.2 copy-done
  8.4 3.6 %maximum_convert_fusion = (bf16[2048,512]{1,0:T(8,128)(2,1)S(1)}, f32[2048,512]{1,0:T(8,128)}) fusion(bf16[2048,256]{1,0:T(8,128)(2,1)S(1)} %bitcast.76, bf16[1,256,512]{2,1,0:T(8,128)(2,1)} %param.9), kind=kOutput, calls=%fused_computation.7 | convolution fusion | flops 538968064 | bytes 7602176 | tf_op jit(solution)/shard_map/dot_general | solution.py:22
  12.0 0.6 fusion.16
  12.8 42.5 %all-gather.2 = f32[16,1,512]{2,1,0:T(1,128)S(1)} all-gather(f32[1,1,512]{2,1,0:T(1,128)S(1)} %bitcast.94), channel_id=2, replica_groups=mesh['depth'=16,'rays'=2] {'depth'}, dimensions={0}, use_global_device_ids=true | all-gather | bytes 34816 | tf_op jit(solution)/shard_map/all_gather | solution.py:41
  55.3 0.1 select_reduce_fusion
  55.4 0.6 fusion.22
  56.1 0.8 fusion.13
  56.8 4.5 %multiply_reduce_fusion.2 = (f32[512,512]{0,1:T(8,128)S(1)}, f32[4,512,512]{1,2,0:T(8,128)}) fusion(f32[4,512]{1,0:T(4,128)S(1)} %subtract_multiply_fusion.1, bf16[4,512,512]{2,1,0:T(8,128)(2,1)S(1)} %bitcast.78, bf16[1,512,512]{2,1,0:T(8,128)(2,1)} %param.10), kind=kOutput, calls=%fused_computation.6 | convolution fusion | flops 1075576832 | bytes 7872512 | tf_op jit(solution)/shard_map/dot_general | solution.py:24
  61.3 1.1 copy-done.2
  62.4 1.1 broadcast_multiply_fusion
  63.6 2.0 copy.25
  65.7 105.6 %all-reduce.3.cloned.1.call-done = f32[512,512]{0,1:T(8,128)} async-done(((f32[512,512]{0,1:T(8,128)}), f32[512,512]{0,1:T(8,128)}) %all-reduce.3.cloned.1.call-update) | async-done | bytes 1048592 | tf_op jit(solution)/shard_map/psum | solution.py:46
  171.3 2.4 multiply_reduce_fusion.3
  173.7 1.4 fusion.2
  175.2 2.2 multiply_reduce_fusion.1
  177.3 4.1 %copy.26 = bf16[4,512,512]{2,1,0:T(8,128)(2,1)} copy(bf16[4,512,512]{1,2,0:T(8,128)(2,1)} %get-tuple-element.27) | data formatting | bytes 4194304 | tf_op jit(solution)/shard_map/convert_element_type | solution.py:54
  181.5 38.9 %all-gather.3 = f32[16,1,512]{2,1,0:T(1,128)S(1)} all-gather(f32[1,1,512]{2,1,0:T(1,128)S(1)} %bitcast.92), channel_id=3, replica_groups=mesh['depth'=16,'rays'=2] {'depth'}, dimensions={0}, use_global_device_ids=true | all-gather | bytes 34816 | tf_op jit(solution)/shard_map/all_gather | solution.py:51
  220.4 0.8 fusion.10
  221.3 5.7 %fusion.1 = bf16[256,512]{0,1:T(8,128)(2,1)S(1)} fusion(bf16[2048,256]{1,0:T(8,128)(2,1)S(1)} %bitcast.77, f32[2048,512]{1,0:T(8,128)} %get-tuple-element.33, bf16[2048,512]{1,0:T(8,128)(2,1)} %bitcast.79, f32[512]{0:T(512)S(1)} %mul.137, f32[2048]{0:T(1024)S(1)} %get-tuple-element.31, bf16[1,512,512]{2,1,0:T(8,128)(2,1)} %param.10), kind=kOutput, calls=%fused_computation.12 | convolution fusion | flops 1615986688 | bytes 8136704 | tf_op jit(solution)/shard_map/dot_general | solution.py:8
  227.0 0.8 copy.31
  227.9 0.0 reduce-scatter.5.cloned.1.call-start
  228.0 2.6 %copy.35 = f32[512,512]{1,0:T(8,128)} copy(f32[512,512]{0,1:T(8,128)} %copy-done.3) | data formatting | bytes 2097152
  230.5 1.6 fusion
  232.1 2.1 convolution_convert_fusion
  234.2 0.6 dynamic-slice
  235.5 3.1 %psum.15 = f32[]{:T(128)} all-reduce(f32[]{:T(128)} %get-tuple-element.24), channel_id=1, replica_groups=mesh['depth'=16,'rays'=2] {'rays'}, use_global_device_ids=true, to_apply=%region_15.16 | all-reduce | flops 1 | bytes 8 | tf_op jit(solution)/shard_map/psum | solution.py:48
  239.2 0.5 multiply_reduce_fusion
  239.7 2.5 all-reduce
  242.2 0.6 dynamic-slice_convert_fusion
  242.8 1.0 copy.32
  243.9 0.8 copy.28
  244.7 1.8 bitcast_convert_fusion
  (42 shorter events, 0.5 us)
Async XLA Ops:
  7.2 1.2 copy-start
  7.2 4.8 %copy-start.5 = (bf16[1,512]{1,0:T(2,128)(2,1)S(1)}, bf16[1,512]{1,0:T(2,128)(2,1)}, u32[]{:S(2)}) copy-start(bf16[1,512]{1,0:T(2,128)(2,1)} %param.11) | copy-start | bytes 3076
  7.2 164.1 %all-reduce.3.cloned.1.call-start = ((), (), s32[]{:S(2)}) async-start(), calls=%async_computation.2 | async-start | bytes 2097152 | tf_op jit(solution)/shard_map/psum | solution.py:46
  8.4 4.3 %copy-start.4 = (f32[1,4,512]{2,1,0:T(4,128)S(1)}, f32[1,4,512]{2,1,0:T(4,128)}, u32[]{:S(2)}) copy-start(f32[1,4,512]{2,1,0:T(4,128)} %param.8) | copy-start | bytes 24580
  8.4 46.9 %copy-start.6 = (s32[1,16]{1,0:T(1,128)S(1)}, s32[1,16]{1,0:T(1,128)}, u32[]{:S(2)}) copy-start(s32[1,16]{1,0:T(1,128)} %param.12) | copy-start | bytes 196
  61.3 1.1 copy-start.2
  63.5 179.3 %reduce-scatter.7.cloned.1.call-start = ((), (), s32[]{:S(2)}) async-start(), calls=%async_computation.4 | async-start | bytes 393216
  171.3 3.8 %copy-start.1 = (f32[4,512,512]{1,2,0:T(8,128)S(1)}, f32[4,512,512]{1,2,0:T(8,128)}, u32[]{:S(2)}) copy-start(f32[4,512,512]{1,2,0:T(8,128)} %get-tuple-element.35) | copy-start | bytes 12582916
  175.2 2.2 copy-start.3
  227.9 16.8 %reduce-scatter.5.cloned.1.call-start = ((), (), s32[]{:S(2)}) async-start(), calls=%async_computation.3 | async-start | bytes 786432 | tf_op jit(solution)/shard_map/reduce_scatter | solution.py:76
  230.5 3.7 %copy-start.7 = (u32[32]{0:T(128)S(1)}, u32[32]{0:T(128)}, u32[]{:S(2)}) copy-start(u32[32]{0:T(128)} %constant.31) | copy-start | bytes 388
Sparse Core Ops, SparseCore 0:
  63.7 107.6 all-reduce.2
  228.0 3.5 reduce-scatter.6
  234.5 9.1 reduce-scatter.4
where the time goes:
time: 255 us; the launch traced here: 254 us
  waiting for transfers between devices  106 us (42%)
  blocking collectives  87 us (34%)
  matrix products  18.1 us (7%)
  between operations  16.3 us (6%)
  local copies, waits for them, and re-layouts  14.3 us (6%)
  other arithmetic  12.6 us (5%)
    psum x1, waiting for transfers between devices, body(): color = lax.psum(weighted, 'depth')  106 us
    all_gather x1, blocking collectives, body(): all_tau = lax.all_gather(depth_tau[None], 'depth', axis=0, tiled=True)  42.5 us
    all_gather x1, blocking collectives, body(): lax.all_gather((trans * qsum)[None], 'depth', axis=0, tiled=True)  38.9 us
    unnamed x28, local copies, waits for them, and re-layouts  10.2 us
    dot_general x2, matrix products, contract_rows(): lax.dot_general(left, right, (((0,), (0,)), ((), ())), preferred_element_...  7.78 us
  transfers between devices with their start and end apart: 3, of which 1 were waited for; matrix products, arithmetic and copies ran while one was open for 5% of the time, Pallas kernels for 0%

commit v1 on v0

v1 whole, which is shorter than its diff:
```python
import functools

import jax
import jax.numpy as jnp
from jax import lax
from jax.experimental import pallas as pl
from jax.experimental.pallas import tpu as pltpu
from jax.sharding import PartitionSpec as P

LANES = 128
PAD_ROWS = 16
TAU_ROWS = 8
MIB = 1024 * 1024
F32 = jnp.float32
BF16 = jnp.bfloat16


def split_parts(value):
    first = value.astype(BF16).astype(F32)
    rest = value - first
    second = rest.astype(BF16).astype(F32)
    return first, second, rest - second


def stack_rows(rows, count):
    out = jnp.concatenate(rows, axis=0)
    if out.shape[0] < count:
        out = jnp.concatenate([out, jnp.zeros((count - out.shape[0], LANES), F32)], axis=0)
    return out


def contract(left, right, dims):
    return lax.dot_general(left, right, (dims, ((), ())), preferred_element_type=F32)


def forward_kernel(
    enc_hbm, delta_hbm, w_in_hbm, w_mid_hbm, w_sig_hbm, send_hbm, stat_hbm,
    enc_ref, delta_ref, w_in_ref, w_mid_ref, w_sig_ref, send_ref, hid_ref, stat_ref, sems, out_sems,
):
    samples, rays = enc_ref.shape[:2]
    blocks = rays // LANES
    chunk = rays // send_ref.shape[0]
    width = w_mid_ref.shape[1]
    copies = [
        pltpu.make_async_copy(w_in_hbm.at[0], w_in_ref, sems.at[0]),
        pltpu.make_async_copy(w_sig_hbm, w_sig_ref, sems.at[1]),
        pltpu.make_async_copy(delta_hbm.at[0], delta_ref, sems.at[2]),
        pltpu.make_async_copy(w_mid_hbm.at[0], w_mid_ref, sems.at[3]),
    ]
    enc_copies = [
        pltpu.make_async_copy(enc_hbm.at[0, k], enc_ref.at[k], sems.at[4 + k]) for k in range(samples)
    ]
    leaving = []

    def leave(source, target):
        leaving.append(pltpu.make_async_copy(source, target, out_sems.at[len(leaving)]))
        leaving[-1].start()

    for copy in [copies[0], enc_copies[0], copies[1], *enc_copies[1:], copies[2], copies[3]]:
        copy.start()
    copies[0].wait()
    copies[1].wait()
    w_in = w_in_ref[...]
    w_sig = w_sig_ref[...].astype(F32)
    lanes = lax.broadcasted_iota(jnp.int32, (rays, LANES), 1)
    pack = jnp.zeros((rays, LANES), F32)
    for k in range(samples):
        enc_copies[k].wait()
        hidden = jnp.maximum(contract(enc_ref[k], w_in, ((1,), (0,))), 0.0).astype(BF16)
        hid_ref[k] = hidden
        pack = jnp.where(lanes == k, jnp.sum(hidden.astype(F32) * w_sig, axis=1, keepdims=True), pack)

    copies[2].wait()
    copies[3].wait()
    tall = [slice(b * LANES, (b + 1) * LANES) for b in range(blocks)]
    logit = jnp.concatenate([pack[at].T[:samples] for at in tall], axis=1)
    spacing = delta_ref[...]
    small = jnp.exp(-jnp.abs(logit))
    tau = (jnp.maximum(logit, 0.0) + jnp.log1p(small)) * spacing
    slope = spacing * jnp.where(logit >= 0, 1.0, small) / (1.0 + small)
    fade = jnp.exp(-tau)
    through = jnp.ones((1, rays), F32)
    total = jnp.zeros((1, rays), F32)
    weights, remains = [], []
    for k in range(samples):
        weights.append(through * (1.0 - fade[k : k + 1]))
        through = through * fade[k : k + 1]
        remains.append(through)
        total = total + tau[k : k + 1]
    lines = jnp.concatenate(weights + remains + [slope], axis=0)
    stat = jnp.concatenate([stack_rows([lines[:, at]], LANES).T for at in tall], axis=0)
    stat_ref[:rays] = stat
    mix = stat[:, 0:1] * hid_ref[0].astype(F32)
    for k in range(1, samples):
        mix = mix + stat[:, k : k + 1] * hid_ref[k].astype(F32)
    mix = mix.astype(BF16)
    stat_ref[rays:] = stack_rows([w_sig[:, t * LANES : (t + 1) * LANES] for t in range(w_sig.shape[1] // LANES)], chunk)
    leave(stat_ref, stat_hbm)
    segment = contract(mix, w_mid_ref[...], ((1,), (0,))).astype(BF16)
    for b in range(blocks):
        tau_rows = stack_rows(list(split_parts(total[:, b * LANES : (b + 1) * LANES])), TAU_ROWS)
        for c in range(LANES // chunk):
            to = b * (LANES // chunk) + c
            for t in range(width // LANES):
                send_ref[to, t * chunk : (t + 1) * chunk] = segment[
                    to * chunk : (to + 1) * chunk, t * LANES : (t + 1) * LANES
                ]
            turned = tau_rows if c == 0 else pltpu.roll(tau_rows, LANES - c * chunk, 1)
            send_ref[to, width // LANES * chunk :] = turned.astype(BF16)
        owners = pl.ds(b * (LANES // chunk), LANES // chunk)
        leave(send_ref.at[owners], send_hbm.at[owners])
    for copy in leaving:
        copy.wait()


def composite_kernel(order_ref, me_ref, got_ref, target_ref, reply_ref, tau_ref, trans_ref, term_ref, gtau_ref):
    del me_ref
    regions = got_ref.shape[0]
    chunk, width = target_ref.shape
    tiles = width // LANES
    fold = regions * chunk // LANES

    for r in range(regions):
        parts = got_ref[r, tiles * chunk :].astype(F32)
        tau_ref[r] = parts[0:1] + parts[1:2] + parts[2:3]
    prefix = jnp.zeros((1, LANES), F32)
    for j in range(regions):
        r = order_ref[0, j]
        trans_ref[r] = jnp.exp(-prefix)
        prefix = prefix + tau_ref[r]
    trans_rows = stack_rows([trans_ref[r] for r in range(regions)], LANES)
    trans = trans_rows.T[:chunk]

    def tile(r, t):
        return got_ref[r, t * chunk : (t + 1) * chunk].astype(F32)

    color = [jnp.zeros((chunk, LANES), F32) for _ in range(tiles)]
    for r in range(regions):
        column = trans[:, r : r + 1]
        for t in range(tiles):
            color[t] = color[t] + column * tile(r, t)
    dcolor = []
    for t in range(tiles):
        err = color[t] - target_ref[:, t * LANES : (t + 1) * LANES].astype(F32)
        dcolor.append(err.astype(BF16))
    dcolor_f = [part.astype(F32) for part in dcolor]
    lanes = lax.broadcasted_iota(jnp.int32, (chunk, LANES), 1)
    terms = jnp.zeros((chunk, LANES), F32)
    for r in range(regions):
        q = tile(r, 0) * dcolor_f[0]
        for t in range(1, tiles):
            q = q + tile(r, t) * dcolor_f[t]
        terms = jnp.where(lanes == r, jnp.sum(q, axis=1, keepdims=True), terms)
    terms = terms * trans
    term_rows = jnp.concatenate([terms, jnp.zeros((LANES - chunk, LANES), F32)], axis=0).T
    for r in range(regions):
        term_ref[r] = term_rows[r : r + 1]
    behind = jnp.zeros((1, LANES), F32)
    for j in reversed(range(regions)):
        r = order_ref[0, j]
        gtau_ref[r] = -behind
        behind = behind + term_ref[r]
    row_lanes = lax.broadcasted_iota(jnp.int32, (fold, LANES), 1)
    extra = []
    for ref in (trans_ref, gtau_ref):
        packed = jnp.zeros((fold, LANES), F32)
        for j in range(regions // fold):
            rows = jnp.concatenate([ref[j * fold + a] for a in range(fold)], axis=0)
            rows = jnp.where(row_lanes < chunk, rows, 0.0)
            packed = packed + (pltpu.roll(rows, j * chunk, 1) if j else rows)
        extra.extend(split_parts(packed)[:2])
    for t in range(tiles):
        reply_ref[t * chunk : (t + 1) * chunk] = dcolor[t]
    reply_ref[tiles * chunk :] = jnp.concatenate(extra, axis=0).astype(BF16)


def backward_kernel(outer, flips, last, place_ref, *refs):
    pieces = sum(1 if flip else outer for flip in flips)
    chunks, refs = refs[:pieces], refs[pieces:]
    enc_ref, stat_ref, w_in_ref, w_mid_ref = refs[:4]
    if last:
        mid_before, in_before, row_before, own_ref, send_ref = refs[4:9]
    else:
        mid_out, in_out, row_out = refs[4:7]
    got_all, enc_all, hid_all, mix_all, stat_all, dpre_all, in_acc, mid_acc = refs[-8:]
    samples, regions, chunk = enc_ref.shape[:3]
    inner = regions // outer
    rays = mix_all.shape[0]
    width = w_mid_ref.shape[2]
    region_me, group_me = place_ref[0], place_ref[1]
    o_me, i_me = lax.div(region_me, inner), lax.rem(region_me, inner)

    tiles = width // LANES
    fold = regions * chunk // LANES
    length = tiles * chunk + 4 * fold
    row_ids = lax.broadcasted_iota(jnp.int32, (fold, LANES), 0)
    mine = row_ids == lax.rem(region_me, fold)
    trans_rows, gtau_rows = [], []
    lane_ids = lax.broadcasted_iota(jnp.int32, (1, LANES), 1)
    squares = row_before[1:2, :LANES] if last else jnp.zeros((1, LANES), F32)
    at, piece = 0, 0
    for flip in flips:
        for shift in range(outer):
            ref, base = (chunks[piece], shift * length) if flip else (chunks[piece + shift], 0)
            square = jnp.zeros((chunk, LANES), F32)
            for t in range(tiles):
                part = ref[base + t * chunk : base + (t + 1) * chunk]
                got_all[at : at + chunk, t * LANES : (t + 1) * LANES] = part
                square = square + part.astype(F32) * part.astype(F32)
            square = jnp.sum(jnp.sum(square, axis=0, keepdims=True), axis=1, keepdims=True)
            extra = ref[base + tiles * chunk : base + length].astype(F32)
            for rows, lo in ((trans_rows, 0), (gtau_rows, 2 * fold)):
                value = extra[lo : lo + fold] + extra[lo + fold : lo + 2 * fold]
                rows.append(jnp.sum(jnp.where(mine, value, 0.0), axis=0, keepdims=True))
            device = lax.rem(o_me + outer - shift, outer) * inner + jnp.bitwise_xor(i_me, flip)
            squares = jnp.where(lane_ids == device, square, squares)
            stat_all[at : at + chunk] = stat_ref[device]
            for k in range(samples):
                enc_all[k * rays + at : k * rays + at + chunk] = enc_ref[k, device]
            at += chunk
        piece += 1 if flip else outer
    hid_all[...] = jnp.maximum(contract(enc_all[...], w_in_ref[0], ((1,), (0,))), 0.0).astype(BF16)

    def columns(rows):
        turn = lax.rem(LANES - lax.div(region_me, fold) * chunk, LANES)
        turned = pltpu.roll(stack_rows(rows, LANES), turn, 1).T
        return jnp.concatenate([turned[:chunk, j : j + 1] for j in range(len(rows))], axis=0)

    trans_all, gtau_all = columns(trans_rows), columns(gtau_rows)
    tail_rows = stat_ref[regions]
    w_sig = jnp.concatenate([tail_rows[t : t + 1] for t in range(hid_all.shape[1] // LANES)], axis=1)
    dcolor = got_all[...]
    turned = contract(dcolor, w_mid_ref[0], ((1,), (1,)))
    block = rays
    spans = [slice(b * block, (b + 1) * block) for b in range(rays // block)]
    lanes = lax.broadcasted_iota(jnp.int32, (block, LANES), 1)
    packed = []
    for at in spans:
        pulled = trans_all[at] * turned[at]
        stat = stat_all[at]
        mix = jnp.zeros(pulled.shape, F32)
        pack = jnp.where(lanes == samples, gtau_all[at], 0.0)
        for k in range(samples):
            hidden = hid_all[k * rays + at.start : k * rays + at.stop].astype(F32)
            mix = mix + stat[:, k : k + 1] * hidden
            pack = jnp.where(lanes == k, jnp.sum(hidden * pulled, axis=1, keepdims=True), pack)
        mix_all[at] = (trans_all[at] * mix).astype(BF16)
        packed.append(pack)

    mid_part = contract(mix_all[...], dcolor, ((0,), (0,)))
    if last:
        mid_acc[...] = mid_part + mid_before[...]
    else:
        mid_out[...] = mid_part

    full = -(-rays // LANES) * LANES
    spill = [jnp.zeros((full - rays, LANES), F32)] if full > rays else []
    dots = jnp.concatenate([*packed, *spill], axis=0)
    stats = jnp.concatenate([stat_all[...], *spill], axis=0)
    tall = [slice(b * LANES, (b + 1) * LANES) for b in range(full // LANES)]
    dots = jnp.concatenate([dots[at].T[:8] for at in tall], axis=1)
    stats = jnp.concatenate([stats[at].T[: 4 * samples] for at in tall], axis=1)
    behind = -dots[samples : samples + 1]
    scales = []
    for k in reversed(range(samples)):
        remain = stats[samples + k : samples + k + 1]
        slope = stats[2 * samples + k : 2 * samples + k + 1]
        scales.insert(0, (remain * dots[k : k + 1] - behind) * slope)
        behind = behind + stats[k : k + 1] * dots[k : k + 1]
    scales = [jnp.concatenate([row[:, at] for row in scales], axis=0) for at in tall]
    scales = jnp.concatenate([stack_rows([part], LANES).T for part in scales], axis=0)

    sig = jnp.zeros((8, hid_all.shape[1]), F32)
    for at in spans:
        pulled = trans_all[at] * turned[at]
        stat, scale = stat_all[at], scales[at]
        for k in range(samples):
            rows = slice(k * rays + at.start, k * rays + at.stop)
            hidden = hid_all[rows].astype(F32)
            dz = scale[:, k : k + 1]
            dpre_all[rows] = jnp.where(hidden > 0, stat[:, k : k + 1] * pulled + dz * w_sig, 0.0).astype(BF16)
            sig = sig + jnp.sum((hidden * dz).reshape(block // 8, 8, -1), axis=0)
    sig = jnp.sum(sig, axis=0, keepdims=True)
    in_part = contract(enc_all[...], dpre_all[...], ((0,), (0,)))
    if not last:
        in_out[...] = in_part
        row_out[0:1] = sig
        row_out[1:2, :LANES] = squares
        return
    in_acc[...] = in_part + in_before[...]
    sig = sig + row_before[0:1]
    loss = jnp.sum(squares, axis=1, keepdims=True)

    groups = send_ref.shape[0] + 1
    e_rows, h_rows = in_acc.shape[0] // groups, mid_acc.shape[0] // groups
    row = lax.broadcasted_iota(jnp.int32, (PAD_ROWS, width), 0)
    tail = jnp.zeros((PAD_ROWS, width), F32)
    for j, part in enumerate(split_parts(jnp.broadcast_to(loss, (PAD_ROWS, width)))):
        tail = jnp.where(row == j + 1, part, tail)

    def fill(ref, at, group):
        ref[at, :e_rows] = in_acc[pl.ds(pl.multiple_of(group * e_rows, e_rows), e_rows), :].astype(BF16)
        ref[at, e_rows : e_rows + h_rows] = mid_acc[
            pl.ds(pl.multiple_of(group * h_rows, h_rows), h_rows), :
        ].astype(BF16)
        mine = sig[:, :h_rows]
        for other in range(1, groups):
            mine = jnp.where(group == other, sig[:, other * h_rows : (other + 1) * h_rows], mine)
        mine = jnp.concatenate([mine, jnp.zeros((1, width - h_rows), F32)], axis=1)
        ref[at, e_rows + h_rows :] = jnp.where(row == 0, mine, tail).astype(BF16)

    fill(own_ref, 0, group_me)
    for shift in range(1, groups):
        fill(send_ref, shift - 1, lax.rem(group_me + shift, groups))


def settle_kernel(scale, *refs):
    parts, (in_ref, mid_ref, sig_ref, loss_ref) = refs[:-4], refs[-4:]
    e_rows, h_rows = in_ref.shape[1], mid_ref.shape[1]

    def added(lo, hi):
        total = parts[0][0, lo:hi].astype(F32)
        for part in parts[1:]:
            total = total + part[0, lo:hi].astype(F32)
        return total

    in_ref[0] = added(0, e_rows)
    mid_ref[0] = added(e_rows, e_rows + h_rows)
    tail = added(e_rows + h_rows, e_rows + h_rows + PAD_ROWS)
    sig_ref[...] = tail[0:1, :h_rows]
    loss_ref[...] = (tail[1:2, :1] + tail[2:3, :1] + tail[3:4, :1]) * scale


def body(encoded, deltas, w_in, w_mid, w_sigma, order, target):
    _, samples, rays_dev, width_in = encoded.shape
    hidden_width, features = w_mid.shape[1:]
    regions, groups = lax.axis_size("depth"), lax.axis_size("rays")
    region_me = lax.axis_index("depth").astype(jnp.int32)
    group_me = lax.axis_index("rays").astype(jnp.int32)
    chunk = rays_dev // regions
    limit = pltpu.CompilerParams(vmem_limit_bytes=24 * MIB)
    vmem, hbm = pl.BlockSpec(memory_space=pltpu.VMEM), pl.BlockSpec(memory_space=pltpu.HBM)

    length = chunk * features // LANES + TAU_ROWS
    payload, stat = pl.pallas_call(
        forward_kernel,
        in_specs=[hbm] * 5,
        out_specs=[hbm] * 2,
        out_shape=[
            jax.ShapeDtypeStruct((regions, length, LANES), BF16),
            jax.ShapeDtypeStruct((rays_dev + chunk, LANES), F32),
        ],
        scratch_shapes=[
            pltpu.VMEM((samples, rays_dev, width_in), BF16),
            pltpu.VMEM((samples, rays_dev), F32),
            pltpu.VMEM((width_in, hidden_width), BF16),
            pltpu.VMEM((hidden_width, features), BF16),
            pltpu.VMEM((1, hidden_width), BF16),
            pltpu.VMEM((regions, length, LANES), BF16),
            pltpu.VMEM((samples, rays_dev, hidden_width), BF16),
            pltpu.VMEM((rays_dev + chunk, LANES), F32),
            pltpu.SemaphoreType.DMA((4 + samples,)),
            pltpu.SemaphoreType.DMA((1 + rays_dev // LANES,)),
        ],
        compiler_params=pltpu.CompilerParams(vmem_limit_bytes=60 * MIB),
        name="forward",
    )(encoded, deltas, w_in, w_mid, w_sigma)

    got = lax.all_to_all(payload, "depth", 0, 0)

    inner = 8
    outer = regions // inner
    fold = rays_dev // LANES
    reply_rows = features // LANES * chunk + 4 * fold
    reply = pl.pallas_call(
        composite_kernel,
        grid_spec=pltpu.PrefetchScalarGridSpec(
            num_scalar_prefetch=2,
            grid=(1,),
            in_specs=[
                pl.BlockSpec((regions, length, LANES), lambda i, order, me: (0, 0, 0)),
                pl.BlockSpec((chunk, features), lambda i, order, me: (me[0], 0)),
            ],
            out_specs=pl.BlockSpec((reply_rows, LANES), lambda i, order, me: (0, 0)),
            scratch_shapes=[pltpu.VMEM((regions, 1, LANES), F32)] * 4,
        ),
        out_shape=jax.ShapeDtypeStruct((reply_rows, LANES), BF16),
        compiler_params=limit,
        name="composite",
    )(order, region_me[None], got, target)

    def hop(value, to):
        return lax.ppermute(value, "depth", [(o * inner + i, to(o, i)) for o in range(outer) for i in range(inner)])

    across = [
        hop(reply, lambda o, i, shift=shift: (o + shift) % outer * inner + i) for shift in range(1, outer)
    ]
    bundle = jnp.concatenate([reply, *across], axis=0)
    turns = [7, 4, 3, 5, 2, 6, 1]
    onward = {}
    for flip in reversed(turns):
        onward[flip] = hop(bundle, lambda o, i, flip=flip: o * inner + (i ^ flip))

    rows = (width_in + hidden_width) // groups + PAD_ROWS
    place = jnp.stack([region_me, group_me])
    shared = (
        encoded.reshape(samples, regions, chunk, width_in),
        stat.reshape(-1, chunk, LANES),
        w_in,
        w_mid,
    )

    def backward(flips, pieces, before, out_shape):
        count = len(flips) * outer * chunk
        return pl.pallas_call(
            functools.partial(backward_kernel, outer, flips, bool(before)),
            in_specs=[pl.BlockSpec(memory_space=pltpu.SMEM)] + [vmem] * (len(pieces) + len(shared) + len(before)),
            out_specs=[vmem] * len(out_shape),
            out_shape=out_shape,
            scratch_shapes=[
                pltpu.VMEM((count, features), BF16),
                pltpu.VMEM((samples * count, width_in), BF16),
                pltpu.VMEM((samples * count, hidden_width), BF16),
                pltpu.VMEM((count, hidden_width), BF16),
                pltpu.VMEM((count, LANES), F32),
                pltpu.VMEM((samples * count, hidden_width), BF16),
                pltpu.VMEM((width_in, hidden_width), F32),
                pltpu.VMEM((hidden_width, features), F32),
            ],
            compiler_params=limit,
            cost_estimate=pl.CostEstimate(
                flops=8 * samples * count * hidden_width * (width_in + features),
                bytes_accessed=2 * samples * count * (width_in + hidden_width),
                transcendentals=0,
            ),
            name="backward_rest" if before else "backward_first",
        )(place, *pieces, *shared, *before)

    early, late = [0, *reversed(turns[:4])], [*reversed(turns[4:])]
    first = backward(
        early,
        [reply, *across, *(onward[flip] for flip in early[1:])],
        [],
        [
            jax.ShapeDtypeStruct((hidden_width, features), F32),
            jax.ShapeDtypeStruct((width_in, hidden_width), F32),
            jax.ShapeDtypeStruct((8, hidden_width), F32),
        ],
    )
    own, send = backward(
        late,
        [onward[flip] for flip in late],
        first,
        [
            jax.ShapeDtypeStruct((1, rows, features), BF16),
            jax.ShapeDtypeStruct((groups - 1, rows, features), BF16),
        ],
    )

    parts = [own]
    for shift in range(1, groups):
        ring = [(g, (g + shift) % groups) for g in range(groups)]
        parts.append(lax.ppermute(send[shift - 1 : shift], "rays", ring))

    e_rows, h_rows = width_in // groups, hidden_width // groups
    grad_in, grad_mid, grad_sigma, loss = pl.pallas_call(
        functools.partial(settle_kernel, 1.0 / (rays_dev * groups * features)),
        out_shape=[
            jax.ShapeDtypeStruct((1, e_rows, hidden_width), F32),
            jax.ShapeDtypeStruct((1, h_rows, features), F32),
            jax.ShapeDtypeStruct((1, h_rows), F32),
            jax.ShapeDtypeStruct((1, 1), F32),
        ],
        compiler_params=limit,
        name="settle",
    )(*parts)
    return (grad_in, grad_mid, grad_sigma, loss[0, 0])


def solution(mesh):
    in_specs = (
        P("depth", None, "rays", None),
        P("depth", None, "rays"),
        P("depth", None, None),
        P("depth", None, None),
        P("depth", None),
        P("rays", None),
        P("rays", None),
    )
    out_specs = (P("depth", "rays", None), P("depth", "rays", None), P("depth", "rays"), P())
    return jax.shard_map(body, mesh=mesh, in_specs=in_specs, out_specs=out_specs, check_vma=False)
```

time: 255 us -> 53.8 us (0.21)
  blocking collectives: 87 us -> 0 us
  waiting for transfers between devices: 106 us -> 21.8 us
  starting transfers between devices: 0.12 us -> 18.7 us
  matrix products: 18.1 us -> 0 us
  between operations: 16.3 us -> 0.75 us
  local copies, waits for them, and re-layouts: 14.3 us -> 0.03 us
  other arithmetic: 12.6 us -> 0.08 us
  Pallas kernels: 0 us -> 12.2 us
    psum x1 -> x0, waiting for transfers between devices: 106 us -> none  [body(): color = lax.psum(weighted, 'depth')]
    all_gather x2 -> x0, blocking collectives: 81.4 us -> none  [the longest x1 42.5 us: body(): all_tau = lax.all_gather(depth_tau[None], 'depth', axis=0, tiled=True)]
    dot_general x7 -> x0, matrix products: 18.1 us -> none  [the longest x2 7.78 us: contract_rows(): lax.dot_general(left, right, (((0,), (0,)), ((), ())), preferred_element_...]
    all_to_all x0 -> x1, waiting for transfers between devices: none -> 15.7 us  [body(): got = lax.all_to_all(payload, 'depth', 0, 0)]
    pallas_call x0 -> x5, Pallas kernels: none -> 12.2 us  [the longest x2 5.49 us: backward(): pl.pallas_call(functools.partial(backward_kernel, outer, flips, bool(befo...]
    ppermute x0 -> x9, starting transfers between devices: none -> 10.3 us  [the longest x8 10.2 us: hop(): lax.ppermute(value, 'depth', [(o * inner + i, to(o, i)) for o in range(ou...]
    unnamed x28 -> x12, local copies, waits for them, and re-layouts: 10.2 us -> 0.03 us
    all_to_all x0 -> x1, starting transfers between devices: none -> 8.44 us  [body(): got = lax.all_to_all(payload, 'depth', 0, 0)]
  transfers between devices with their start and end apart: 3 -> 10, of which waited for: 1 -> 5; matrix products, arithmetic and copies ran while one was open for 5% -> 0% of each run, Pallas kernels for 0% -> 6%
where the time goes in v1:
time: 53.8 us; the launch traced here: 53.6 us
  waiting for transfers between devices  21.8 us (41%)
  starting transfers between devices  18.7 us (35%)
  Pallas kernels  12.2 us (23%)
  between operations  0.75 us (1%)
    all_to_all x1, waiting for transfers between devices, body(): got = lax.all_to_all(payload, 'depth', 0, 0)  15.7 us
    ppermute x8, starting transfers between devices, hop(): lax.ppermute(value, 'depth', [(o * inner + i, to(o, i)) for o in range(ou...  10.2 us
    all_to_all x1, starting transfers between devices, body(): got = lax.all_to_all(payload, 'depth', 0, 0)  8.44 us
    pallas_call x2, Pallas kernels, backward(): pl.pallas_call(functools.partial(backward_kernel, outer, flips, bool(befo...  5.49 us
    pallas_call x1, Pallas kernels, body(): pl.pallas_call(forward_kernel, in_specs=[hbm] * 5, out_specs=[hbm] * 2, o...  4.51 us
    ppermute x8, waiting for transfers between devices, hop(): lax.ppermute(value, 'depth', [(o * inner + i, to(o, i)) for o in range(ou...  4.4 us
    ppermute x1, waiting for transfers between devices, body(): parts.append(lax.ppermute(send[shift - 1:shift], 'rays', ring))  1.73 us
    pallas_call x1, Pallas kernels, body(): pl.pallas_call(composite_kernel, grid_spec=pltpu.PrefetchScalarGridSpec(n...  1.21 us
  transfers between devices with their start and end apart: 10, of which 5 were waited for; matrix products, arithmetic and copies ran while one was open for 0% of the time, Pallas kernels for 6%

profile of v1, /device:TPU:0, one launch (start us, length us, event | category | flops | bytes accessed | tf_op | source)
XLA Modules:
  0.0 53.6 jit_solution(18067017731429922638)
XLA Ops:
  0.6 4.5 %forward.1 = (bf16[16,136,128]{2,1,0:T(8,128)(2,1)}, f32[544,128]{1,0:T(8,128)}) custom-call(bf16[1,4,512,256]{3,2,1,0:T(8,128)(2,1)} %enc_hbm.1, f32[1,4,512]{2,1,0:T(4,128)} %delta_hbm.1, bf16[1,256,512]{2,1,0:T(8,128)(2,1)} %refs_5_.1, bf16[1,512,512]{2,1,0:T(8,128)(2,1)} %refs_6_.1, bf16[1,512]{1,0:T(2,128)(2,1)} %w_sig_hbm.1), custom_call_target="tpu_custom_call" | custom-call | tf_op jit(solution)/shard_map/forward/pallas_call | solution.py:345
  5.2 0.0 copy-start
  5.2 8.4 %all-to-all-start = ((bf16[16,136,128]{2,1,0:T(8,128)(2,1)}), bf16[16,136,128]{2,1,0:T(8,128)(2,1)S(1)}, u32[]{:S(2)}, u32[]{:S(2)}) async-start(bf16[16,136,128]{2,1,0:T(8,128)(2,1)} %get-tuple-element.15), calls=%async_computation | async-start | bytes 1114112 | tf_op jit(solution)/shard_map/all_to_all | solution.py:369
  13.6 0.0 copy-start.4
  13.6 15.7 %all-to-all-done.got_ref = bf16[16,136,128]{2,1,0:T(8,128)(2,1)S(1)} async-done(((bf16[16,136,128]{2,1,0:T(8,128)(2,1)}), bf16[16,136,128]{2,1,0:T(8,128)(2,1)S(1)}, u32[]{:S(2)}, u32[]{:S(2)}) %all-to-all-start) | async-done | bytes 557088 | tf_op jit(solution)/shard_map/all_to_all | solution.py:369
  29.3 0.0 copy-done.4
  29.4 0.0 copy-start.5
  29.4 1.2 %composite.1.refs_0_ = bf16[144,128]{1,0:T(8,128)(2,1)S(1)} custom-call(s32[1,16]{1,0:T(1,128)S(1)} %copy-done.4, s32[1]{0:T(128)} %bitcast.me_ref, bf16[16,136,128]{2,1,0:T(8,128)(2,1)S(1)} %all-to-all-done.got_ref, bf16[512,512]{1,0:T(8,128)(2,1)S(1)} %copy-done.1), custom_call_target="tpu_custom_call" | custom-call | tf_op jit(solution)/shard_map/composite/pallas_call | solution.py:375
  30.6 0.9 %collective-permute-start = (bf16[144,128]{1,0:T(8,128)(2,1)S(1)}, bf16[144,128]{1,0:T(8,128)(2,1)S(1)}, u32[]{:S(2)}, u32[]{:S(2)}) collective-permute-start(bf16[144,128]{1,0:T(8,128)(2,1)S(1)} %composite.1.refs_0_), channel_id=1, source_target_pairs={{0,16},{2,18},{4,20},{6,22},{8,24},{10,26},{12,28},{14,30},{16,0},... | collective-permute-start | bytes 110600 | tf_op jit(solution)/shard_map/ppermute | solution.py:393
  31.4 4.0 %collective-permute-done.refs_1_ = bf16[144,128]{1,0:T(8,128)(2,1)S(1)} collective-permute-done((bf16[144,128]{1,0:T(8,128)(2,1)S(1)}, bf16[144,128]{1,0:T(8,128)(2,1)S(1)}, u32[]{:S(2)}, u32[]{:S(2)}) %collective-permute-start) | collective-permute-done | bytes 36896 | tf_op jit(solution)/shard_map/ppermute | solution.py:393
  35.5 1.7 %collective-permute-start.7 = (bf16[288,128]{1,0:T(8,128)(2,1)S(1)}, bf16[288,128]{1,0:T(8,128)(2,1)S(1)}, u32[]{:S(2)}, u32[]{:S(2)}) collective-permute-start(bf16[288,128]{1,0:T(8,128)(2,1)S(1)} %pad_maximum_fusion), channel_id=1, source_target_pairs={{0,14},{2,12},{4,10},{6,8},{8,6},{10,4},{12,2},{14,0},{16,30},{18,... | collective-permute-start | bytes 221192 | tf_op jit(solution)/shard_map/ppermute | solution.py:393
  37.2 0.7 %collective-permute-start.6 = (bf16[288,128]{1,0:T(8,128)(2,1)S(1)}, bf16[288,128]{1,0:T(8,128)(2,1)S(1)}, u32[]{:S(2)}, u32[]{:S(2)}) collective-permute-start(bf16[288,128]{1,0:T(8,128)(2,1)S(1)} %pad_maximum_fusion), channel_id=1, source_target_pairs={{0,8},{2,10},{4,12},{6,14},{8,0},{10,2},{12,4},{14,6},{16,24},{18,... | collective-permute-start | bytes 221192 | tf_op jit(solution)/shard_map/ppermute | solution.py:393
  37.9 1.9 %collective-permute-start.5 = (bf16[288,128]{1,0:T(8,128)(2,1)S(1)}, bf16[288,128]{1,0:T(8,128)(2,1)S(1)}, u32[]{:S(2)}, u32[]{:S(2)}) collective-permute-start(bf16[288,128]{1,0:T(8,128)(2,1)S(1)} %pad_maximum_fusion), channel_id=1, source_target_pairs={{0,6},{2,4},{4,2},{6,0},{8,14},{10,12},{12,10},{14,8},{16,22},{18,... | collective-permute-start | bytes 221192 | tf_op jit(solution)/shard_map/ppermute | solution.py:393
  39.8 1.4 %collective-permute-start.4 = (bf16[288,128]{1,0:T(8,128)(2,1)S(1)}, bf16[288,128]{1,0:T(8,128)(2,1)S(1)}, u32[]{:S(2)}, u32[]{:S(2)}) collective-permute-start(bf16[288,128]{1,0:T(8,128)(2,1)S(1)} %pad_maximum_fusion), channel_id=1, source_target_pairs={{0,10},{2,8},{4,14},{6,12},{8,2},{10,0},{12,6},{14,4},{16,26},{18,... | collective-permute-start | bytes 221192 | tf_op jit(solution)/shard_map/ppermute | solution.py:393
  41.2 0.1 pad_add_fusion.place_ref
  41.3 0.9 %collective-permute-start.3 = (bf16[288,128]{1,0:T(8,128)(2,1)S(1)}, bf16[288,128]{1,0:T(8,128)(2,1)S(1)}, u32[]{:S(2)}, u32[]{:S(2)}) collective-permute-start(bf16[288,128]{1,0:T(8,128)(2,1)S(1)} %pad_maximum_fusion), channel_id=1, source_target_pairs={{0,4},{2,6},{4,0},{6,2},{8,12},{10,14},{12,8},{14,10},{16,20},{18,... | collective-permute-start | bytes 221192 | tf_op jit(solution)/shard_map/ppermute | solution.py:393
  42.2 0.0 collective-permute-done.7.refs_5_
  42.2 1.8 %collective-permute-start.2 = (bf16[288,128]{1,0:T(8,128)(2,1)S(1)}, bf16[288,128]{1,0:T(8,128)(2,1)S(1)}, u32[]{:S(2)}, u32[]{:S(2)}) collective-permute-start(bf16[288,128]{1,0:T(8,128)(2,1)S(1)} %pad_maximum_fusion), channel_id=1, source_target_pairs={{0,12},{2,14},{4,8},{6,10},{8,4},{10,6},{12,0},{14,2},{16,28},{18,... | collective-permute-start | bytes 221192 | tf_op jit(solution)/shard_map/ppermute | solution.py:393
  44.1 0.0 collective-permute-done.6.refs_4_
  44.1 0.8 %collective-permute-start.1 = (bf16[288,128]{1,0:T(8,128)(2,1)S(1)}, bf16[288,128]{1,0:T(8,128)(2,1)S(1)}, u32[]{:S(2)}, u32[]{:S(2)}) collective-permute-start(bf16[288,128]{1,0:T(8,128)(2,1)S(1)} %pad_maximum_fusion), channel_id=1, source_target_pairs={{0,2},{2,0},{4,6},{6,4},{8,10},{10,8},{12,14},{14,12},{16,18},{18,... | collective-permute-start | bytes 221192 | tf_op jit(solution)/shard_map/ppermute | solution.py:393
  44.9 0.0 collective-permute-done.5.refs_3_
  44.9 0.2 collective-permute-done.4.refs_2_
  45.1 0.0 copy-done.3
  45.1 0.0 copy-done.5
  45.1 3.1 %backward_first.1 = (f32[512,512]{1,0:T(8,128)S(1)}, f32[256,512]{1,0:T(8,128)S(1)}, f32[8,512]{1,0:T(8,128)S(1)}) custom-call(s32[2]{0:T(128)S(1)} %pad_add_fusion.place_ref, bf16[144,128]{1,0:T(8,128)(2,1)S(1)} %composite.1.refs_0_, bf16[144,128]{1,0:T(8,128)(2,1)S(1)} %collective-permute-done.refs_1_, ...), custom_call_target="tpu_custom_call" | custom-call | flops 4026531840 | bytes 1966080 | tf_op jit(solution)/shard_map/backward_first/pallas_call | solution.py:415
  48.2 0.0 collective-permute-done.3.refs_2_
  48.2 0.0 collective-permute-done.2.refs_1_
  48.3 0.2 collective-permute-done.1.refs_0_
  48.4 2.4 %backward_rest.1 = (bf16[1,400,512]{2,1,0:T(8,128)(2,1)S(1)}, bf16[1,400,512]{2,1,0:T(8,128)(2,1)S(1)}) custom-call(s32[2]{0:T(128)S(1)} %pad_add_fusion.place_ref, bf16[288,128]{1,0:T(8,128)(2,1)S(1)} %collective-permute-done.1.refs_0_, bf16[288,128]{1,0:T(8,128)(2,1)S(1)} %collective-permute-done.2.refs_1_, ...), custom_call_target="tpu_custom_call" | custom-call | flops 2415919104 | bytes 1179648 | tf_op jit(solution)/shard_map/backward_rest/pallas_call | solution.py:415
  50.8 0.1 collective-permute-start.8
  50.9 1.7 %collective-permute-done.8.refs_1_ = bf16[1,400,512]{2,1,0:T(8,128)(2,1)S(1)} collective-permute-done((bf16[1,400,512]{2,1,0:T(8,128)(2,1)S(1)}, bf16[1,400,512]{2,1,0:T(8,128)(2,1)S(1)}, u32[]{:S(2)}, u32[]{:S(2)}) %collective-permute-start.8) | collective-permute-done | bytes 409632 | tf_op jit(solution)/shard_map/ppermute | solution.py:463
  52.6 1.0 %settle.1 = (f32[1,128,512]{2,1,0:T(8,128)}, f32[1,256,512]{2,1,0:T(8,128)}, f32[1,256]{1,0:T(1,128)}, f32[1,1]{1,0:T(1,128)}) custom-call(bf16[1,400,512]{2,1,0:T(8,128)(2,1)S(1)} %get-tuple-element.20.refs_0_, bf16[1,400,512]{2,1,0:T(8,128)(2,1)S(1)} %collective-permute-done.8.refs_1_), custom_call_target="tpu_custom_call" | custom-call | tf_op jit(solution)/shard_map/settle/pallas_call | solution.py:466
  (7 shorter events, 0.0 us)
Async XLA Ops:
  0.6 28.7 %copy-start.1 = (bf16[512,512]{1,0:T(8,128)(2,1)S(1)}, bf16[512,512]{1,0:T(8,128)(2,1)}, u32[]{:S(2)}) copy-start(bf16[512,512]{1,0:T(8,128)(2,1)} %target_ref.1) | copy-start | bytes 1572868
  5.2 39.9 %copy-start = (bf16[1,4,512,256]{3,2,1,0:T(8,128)(2,1)S(1)}, bf16[1,4,512,256]{3,2,1,0:T(8,128)(2,1)}, u32[]{:S(2)}) copy-start(bf16[1,4,512,256]{3,2,1,0:T(8,128)(2,1)} %enc_hbm.1) | copy-start | bytes 3145732
  5.2 24.2 %all-to-all-start = ((bf16[16,136,128]{2,1,0:T(8,128)(2,1)}), bf16[16,136,128]{2,1,0:T(8,128)(2,1)S(1)}, u32[]{:S(2)}, u32[]{:S(2)}) async-start(bf16[16,136,128]{2,1,0:T(8,128)(2,1)} %get-tuple-element.15), calls=%async_computation | async-start | bytes 1114112 | tf_op jit(solution)/shard_map/all_to_all | solution.py:369
  13.6 15.7 %copy-start.4 = (s32[1,16]{1,0:T(1,128)S(1)}, s32[1,16]{1,0:T(1,128)}, u32[]{:S(2)}) copy-start(s32[1,16]{1,0:T(1,128)} %order_ref.1) | copy-start | bytes 196
  29.3 15.8 %copy-start.2 = (bf16[1,512,512]{2,1,0:T(8,128)(2,1)S(1)}, bf16[1,512,512]{2,1,0:T(8,128)(2,1)}, u32[]{:S(2)}) copy-start(bf16[1,512,512]{2,1,0:T(8,128)(2,1)} %refs_6_.1) | copy-start | bytes 1572868
  29.3 15.8 %copy-start.3 = (bf16[1,256,512]{2,1,0:T(8,128)(2,1)S(1)}, bf16[1,256,512]{2,1,0:T(8,128)(2,1)}, u32[]{:S(2)}) copy-start(bf16[1,256,512]{2,1,0:T(8,128)(2,1)} %refs_5_.1) | copy-start | bytes 786436
  29.4 15.8 %copy-start.5 = (f32[544,128]{1,0:T(8,128)S(1)}, f32[544,128]{1,0:T(8,128)}, u32[]{:S(2)}) copy-start(f32[544,128]{1,0:T(8,128)} %get-tuple-element.16) | copy-start | bytes 835588
  30.6 4.9 %collective-permute-start = (bf16[144,128]{1,0:T(8,128)(2,1)S(1)}, bf16[144,128]{1,0:T(8,128)(2,1)S(1)}, u32[]{:S(2)}, u32[]{:S(2)}) collective-permute-start(bf16[144,128]{1,0:T(8,128)(2,1)S(1)} %composite.1.refs_0_), channel_id=1, source_target_pairs={{0,16},{2,18},{4,20},{6,22},{8,24},{10,26},{12,28},{14,30},{16,0},... | collective-permute-start | bytes 110600 | tf_op jit(solution)/shard_map/ppermute | solution.py:393
  35.5 6.8 %collective-permute-start.7 = (bf16[288,128]{1,0:T(8,128)(2,1)S(1)}, bf16[288,128]{1,0:T(8,128)(2,1)S(1)}, u32[]{:S(2)}, u32[]{:S(2)}) collective-permute-start(bf16[288,128]{1,0:T(8,128)(2,1)S(1)} %pad_maximum_fusion), channel_id=1, source_target_pairs={{0,14},{2,12},{4,10},{6,8},{8,6},{10,4},{12,2},{14,0},{16,30},{18,... | collective-permute-start | bytes 221192 | tf_op jit(solution)/shard_map/ppermute | solution.py:393
  37.2 6.9 %collective-permute-start.6 = (bf16[288,128]{1,0:T(8,128)(2,1)S(1)}, bf16[288,128]{1,0:T(8,128)(2,1)S(1)}, u32[]{:S(2)}, u32[]{:S(2)}) collective-permute-start(bf16[288,128]{1,0:T(8,128)(2,1)S(1)} %pad_maximum_fusion), channel_id=1, source_target_pairs={{0,8},{2,10},{4,12},{6,14},{8,0},{10,2},{12,4},{14,6},{16,24},{18,... | collective-permute-start | bytes 221192 | tf_op jit(solution)/shard_map/ppermute | solution.py:393
  37.9 7.0 %collective-permute-start.5 = (bf16[288,128]{1,0:T(8,128)(2,1)S(1)}, bf16[288,128]{1,0:T(8,128)(2,1)S(1)}, u32[]{:S(2)}, u32[]{:S(2)}) collective-permute-start(bf16[288,128]{1,0:T(8,128)(2,1)S(1)} %pad_maximum_fusion), channel_id=1, source_target_pairs={{0,6},{2,4},{4,2},{6,0},{8,14},{10,12},{12,10},{14,8},{16,22},{18,... | collective-permute-start | bytes 221192 | tf_op jit(solution)/shard_map/ppermute | solution.py:393
  39.8 5.3 %collective-permute-start.4 = (bf16[288,128]{1,0:T(8,128)(2,1)S(1)}, bf16[288,128]{1,0:T(8,128)(2,1)S(1)}, u32[]{:S(2)}, u32[]{:S(2)}) collective-permute-start(bf16[288,128]{1,0:T(8,128)(2,1)S(1)} %pad_maximum_fusion), channel_id=1, source_target_pairs={{0,10},{2,8},{4,14},{6,12},{8,2},{10,0},{12,6},{14,4},{16,26},{18,... | collective-permute-start | bytes 221192 | tf_op jit(solution)/shard_map/ppermute | solution.py:393
  41.3 7.0 %collective-permute-start.3 = (bf16[288,128]{1,0:T(8,128)(2,1)S(1)}, bf16[288,128]{1,0:T(8,128)(2,1)S(1)}, u32[]{:S(2)}, u32[]{:S(2)}) collective-permute-start(bf16[288,128]{1,0:T(8,128)(2,1)S(1)} %pad_maximum_fusion), channel_id=1, source_target_pairs={{0,4},{2,6},{4,0},{6,2},{8,12},{10,14},{12,8},{14,10},{16,20},{18,... | collective-permute-start | bytes 221192 | tf_op jit(solution)/shard_map/ppermute | solution.py:393
  42.2 6.0 %collective-permute-start.2 = (bf16[288,128]{1,0:T(8,128)(2,1)S(1)}, bf16[288,128]{1,0:T(8,128)(2,1)S(1)}, u32[]{:S(2)}, u32[]{:S(2)}) collective-permute-start(bf16[288,128]{1,0:T(8,128)(2,1)S(1)} %pad_maximum_fusion), channel_id=1, source_target_pairs={{0,12},{2,14},{4,8},{6,10},{8,4},{10,6},{12,0},{14,2},{16,28},{18,... | collective-permute-start | bytes 221192 | tf_op jit(solution)/shard_map/ppermute | solution.py:393
  44.1 4.4 %collective-permute-start.1 = (bf16[288,128]{1,0:T(8,128)(2,1)S(1)}, bf16[288,128]{1,0:T(8,128)(2,1)S(1)}, u32[]{:S(2)}, u32[]{:S(2)}) collective-permute-start(bf16[288,128]{1,0:T(8,128)(2,1)S(1)} %pad_maximum_fusion), channel_id=1, source_target_pairs={{0,2},{2,0},{4,6},{6,4},{8,10},{10,8},{12,14},{14,12},{16,18},{18,... | collective-permute-start | bytes 221192 | tf_op jit(solution)/shard_map/ppermute | solution.py:393
  50.8 1.8 %collective-permute-start.8 = (bf16[1,400,512]{2,1,0:T(8,128)(2,1)S(1)}, bf16[1,400,512]{2,1,0:T(8,128)(2,1)S(1)}, u32[]{:S(2)}, u32[]{:S(2)}) collective-permute-start(bf16[1,400,512]{2,1,0:T(8,128)(2,1)S(1)} %get-tuple-element.21), channel_id=1, source_target_pairs={{0,1},{1,0},{2,3},{3,2},{4,5},{5,4},{6,7},{7,6},{8,9},{9,8},{10,11... | collective-permute-start | bytes 1228808 | tf_op jit(solution)/shard_map/ppermute | solution.py:463

commit v2 on v1

--- a/solution.py
+++ b/solution.py
@@ -231,21 +231,17 @@
     w_sig = jnp.concatenate([tail_rows[t : t + 1] for t in range(hid_all.shape[1] // LANES)], axis=1)
     dcolor = got_all[...]
     turned = contract(dcolor, w_mid_ref[0], ((1,), (1,)))
-    block = rays
-    spans = [slice(b * block, (b + 1) * block) for b in range(rays // block)]
-    lanes = lax.broadcasted_iota(jnp.int32, (block, LANES), 1)
-    packed = []
-    for at in spans:
-        pulled = trans_all[at] * turned[at]
-        stat = stat_all[at]
-        mix = jnp.zeros(pulled.shape, F32)
-        pack = jnp.where(lanes == samples, gtau_all[at], 0.0)
-        for k in range(samples):
-            hidden = hid_all[k * rays + at.start : k * rays + at.stop].astype(F32)
-            mix = mix + stat[:, k : k + 1] * hidden
-            pack = jnp.where(lanes == k, jnp.sum(hidden * pulled, axis=1, keepdims=True), pack)
-        mix_all[at] = (trans_all[at] * mix).astype(BF16)
-        packed.append(pack)
+    pulled = trans_all * turned
+    stat = stat_all[...]
+    lanes = lax.broadcasted_iota(jnp.int32, (rays, LANES), 1)
+    hidden = hid_all[...].astype(F32).reshape(samples, rays, -1)
+    sums = jnp.sum(hidden * pulled[None], axis=2, keepdims=True)
+    packed = jnp.where(lanes == samples, gtau_all, 0.0)
+    mix = jnp.zeros(pulled.shape, F32)
+    for k in range(samples):
+        mix = mix + stat[:, k : k + 1] * hidden[k]
+        packed = jnp.where(lanes == k, sums[k], packed)
+    mix_all[...] = (trans_all * mix).astype(BF16)
 
     mid_part = contract(mix_all[...], dcolor, ((0,), (0,)))
     if last:
@@ -255,8 +251,8 @@
 
     full = -(-rays // LANES) * LANES
     spill = [jnp.zeros((full - rays, LANES), F32)] if full > rays else []
-    dots = jnp.concatenate([*packed, *spill], axis=0)
-    stats = jnp.concatenate([stat_all[...], *spill], axis=0)
+    dots = jnp.concatenate([packed, *spill], axis=0)
+    stats = jnp.concatenate([stat, *spill], axis=0)
     tall = [slice(b * LANES, (b + 1) * LANES) for b in range(full // LANES)]
     dots = jnp.concatenate([dots[at].T[:8] for at in tall], axis=1)
     stats = jnp.concatenate([stats[at].T[: 4 * samples] for at in tall], axis=1)
@@ -271,15 +267,12 @@
     scales = jnp.concatenate([stack_rows([part], LANES).T for part in scales], axis=0)
 
     sig = jnp.zeros((8, hid_all.shape[1]), F32)
-    for at in spans:
-        pulled = trans_all[at] * turned[at]
-        stat, scale = stat_all[at], scales[at]
-        for k in range(samples):
-            rows = slice(k * rays + at.start, k * rays + at.stop)
-            hidden = hid_all[rows].astype(F32)
-            dz = scale[:, k : k + 1]
-            dpre_all[rows] = jnp.where(hidden > 0, stat[:, k : k + 1] * pulled + dz * w_sig, 0.0).astype(BF16)
-            sig = sig + jnp.sum((hidden * dz).reshape(block // 8, 8, -1), axis=0)
+    for k in range(samples):
+        rows = slice(k * rays, (k + 1) * rays)
+        hidden = hid_all[rows].astype(F32)
+        dz = scales[:rays, k : k + 1]
+        dpre_all[rows] = jnp.where(hidden > 0, stat[:, k : k + 1] * pulled + dz * w_sig, 0.0).astype(BF16)
+        sig = sig + jnp.sum((hidden * dz).reshape(rays // 8, 8, -1), axis=0)
     sig = jnp.sum(sig, axis=0, keepdims=True)
     in_part = contract(enc_all[...], dpre_all[...], ((0,), (0,)))
     if not last:

time: 53.8 us -> 53.8 us (level)
  no operation moved by 1% of the time
where the time goes in v2:
time: 53.8 us; the launch traced here: 53.5 us
  waiting for transfers between devices  21.8 us (41%)
  starting transfers between devices  18.7 us (35%)
  Pallas kernels  12.1 us (22%)
  between operations  0.75 us (1%)
    all_to_all x1, waiting for transfers between devices, body(): got = lax.all_to_all(payload, 'depth', 0, 0)  15.7 us
    ppermute x8, starting transfers between devices, hop(): lax.ppermute(value, 'depth', [(o * inner + i, to(o, i)) for o in range(ou...  10.2 us
    all_to_all x1, starting transfers between devices, body(): got = lax.all_to_all(payload, 'depth', 0, 0)  8.44 us
    pallas_call x2, Pallas kernels, backward(): pl.pallas_call(functools.partial(backward_kernel, outer, flips, bool(befo...  5.42 us
    pallas_call x1, Pallas kernels, body(): pl.pallas_call(forward_kernel, in_specs=[hbm] * 5, out_specs=[hbm] * 2, o...  4.51 us
    ppermute x8, waiting for transfers between devices, hop(): lax.ppermute(value, 'depth', [(o * inner + i, to(o, i)) for o in range(ou...  4.42 us
    ppermute x1, waiting for transfers between devices, body(): parts.append(lax.ppermute(send[shift - 1:shift], 'rays', ring))  1.73 us
    pallas_call x1, Pallas kernels, body(): pl.pallas_call(composite_kernel, grid_spec=pltpu.PrefetchScalarGridSpec(n...  1.21 us
  transfers between devices with their start and end apart: 10, of which 5 were waited for; matrix products, arithmetic and copies ran while one was open for 0% of the time, Pallas kernels for 6%

profile of v2, /device:TPU:0, one launch (start us, length us, event | category | flops | bytes accessed | tf_op | source)
XLA Modules:
  0.0 53.5 jit_solution(7239809578281283139)
XLA Ops:
  0.6 0.0 copy-start.1
  0.6 4.5 %forward.1 = (bf16[16,136,128]{2,1,0:T(8,128)(2,1)}, f32[544,128]{1,0:T(8,128)}) custom-call(bf16[1,4,512,256]{3,2,1,0:T(8,128)(2,1)} %enc_hbm.1, f32[1,4,512]{2,1,0:T(4,128)} %delta_hbm.1, bf16[1,256,512]{2,1,0:T(8,128)(2,1)} %refs_5_.1, bf16[1,512,512]{2,1,0:T(8,128)(2,1)} %refs_6_.1, bf16[1,512]{1,0:T(2,128)(2,1)} %w_sig_hbm.1), custom_call_target="tpu_custom_call" | custom-call | tf_op jit(solution)/shard_map/forward/pallas_call | solution.py:338
  5.2 0.0 copy-start
  5.2 8.4 %all-to-all-start = ((bf16[16,136,128]{2,1,0:T(8,128)(2,1)}), bf16[16,136,128]{2,1,0:T(8,128)(2,1)S(1)}, u32[]{:S(2)}, u32[]{:S(2)}) async-start(bf16[16,136,128]{2,1,0:T(8,128)(2,1)} %get-tuple-element.15), calls=%async_computation | async-start | bytes 1114112 | tf_op jit(solution)/shard_map/all_to_all | solution.py:362
  13.6 0.0 copy-start.4
  13.6 15.7 %all-to-all-done.got_ref = bf16[16,136,128]{2,1,0:T(8,128)(2,1)S(1)} async-done(((bf16[16,136,128]{2,1,0:T(8,128)(2,1)}), bf16[16,136,128]{2,1,0:T(8,128)(2,1)S(1)}, u32[]{:S(2)}, u32[]{:S(2)}) %all-to-all-start) | async-done | bytes 557088 | tf_op jit(solution)/shard_map/all_to_all | solution.py:362
  29.3 0.0 copy-done.1
  29.4 0.0 copy-start.5
  29.4 1.2 %composite.1.refs_0_ = bf16[144,128]{1,0:T(8,128)(2,1)S(1)} custom-call(s32[1,16]{1,0:T(1,128)S(1)} %copy-done.4, s32[1]{0:T(128)} %bitcast.me_ref, bf16[16,136,128]{2,1,0:T(8,128)(2,1)S(1)} %all-to-all-done.got_ref, bf16[512,512]{1,0:T(8,128)(2,1)S(1)} %copy-done.1), custom_call_target="tpu_custom_call" | custom-call | tf_op jit(solution)/shard_map/composite/pallas_call | solution.py:368
  30.6 0.9 %collective-permute-start = (bf16[144,128]{1,0:T(8,128)(2,1)S(1)}, bf16[144,128]{1,0:T(8,128)(2,1)S(1)}, u32[]{:S(2)}, u32[]{:S(2)}) collective-permute-start(bf16[144,128]{1,0:T(8,128)(2,1)S(1)} %composite.1.refs_0_), channel_id=1, source_target_pairs={{0,16},{2,18},{4,20},{6,22},{8,24},{10,26},{12,28},{14,30},{16,0},... | collective-permute-start | bytes 110600 | tf_op jit(solution)/shard_map/ppermute | solution.py:386
  31.4 4.0 %collective-permute-done.refs_1_ = bf16[144,128]{1,0:T(8,128)(2,1)S(1)} collective-permute-done((bf16[144,128]{1,0:T(8,128)(2,1)S(1)}, bf16[144,128]{1,0:T(8,128)(2,1)S(1)}, u32[]{:S(2)}, u32[]{:S(2)}) %collective-permute-start) | collective-permute-done | bytes 36896 | tf_op jit(solution)/shard_map/ppermute | solution.py:386
  35.5 1.7 %collective-permute-start.7 = (bf16[288,128]{1,0:T(8,128)(2,1)S(1)}, bf16[288,128]{1,0:T(8,128)(2,1)S(1)}, u32[]{:S(2)}, u32[]{:S(2)}) collective-permute-start(bf16[288,128]{1,0:T(8,128)(2,1)S(1)} %pad_maximum_fusion), channel_id=1, source_target_pairs={{0,14},{2,12},{4,10},{6,8},{8,6},{10,4},{12,2},{14,0},{16,30},{18,... | collective-permute-start | bytes 221192 | tf_op jit(solution)/shard_map/ppermute | solution.py:386
  37.2 0.7 %collective-permute-start.6 = (bf16[288,128]{1,0:T(8,128)(2,1)S(1)}, bf16[288,128]{1,0:T(8,128)(2,1)S(1)}, u32[]{:S(2)}, u32[]{:S(2)}) collective-permute-start(bf16[288,128]{1,0:T(8,128)(2,1)S(1)} %pad_maximum_fusion), channel_id=1, source_target_pairs={{0,8},{2,10},{4,12},{6,14},{8,0},{10,2},{12,4},{14,6},{16,24},{18,... | collective-permute-start | bytes 221192 | tf_op jit(solution)/shard_map/ppermute | solution.py:386
  37.9 1.9 %collective-permute-start.5 = (bf16[288,128]{1,0:T(8,128)(2,1)S(1)}, bf16[288,128]{1,0:T(8,128)(2,1)S(1)}, u32[]{:S(2)}, u32[]{:S(2)}) collective-permute-start(bf16[288,128]{1,0:T(8,128)(2,1)S(1)} %pad_maximum_fusion), channel_id=1, source_target_pairs={{0,6},{2,4},{4,2},{6,0},{8,14},{10,12},{12,10},{14,8},{16,22},{18,... | collective-permute-start | bytes 221192 | tf_op jit(solution)/shard_map/ppermute | solution.py:386
  39.8 1.4 %collective-permute-start.4 = (bf16[288,128]{1,0:T(8,128)(2,1)S(1)}, bf16[288,128]{1,0:T(8,128)(2,1)S(1)}, u32[]{:S(2)}, u32[]{:S(2)}) collective-permute-start(bf16[288,128]{1,0:T(8,128)(2,1)S(1)} %pad_maximum_fusion), channel_id=1, source_target_pairs={{0,10},{2,8},{4,14},{6,12},{8,2},{10,0},{12,6},{14,4},{16,26},{18,... | collective-permute-start | bytes 221192 | tf_op jit(solution)/shard_map/ppermute | solution.py:386
  41.2 0.1 pad_add_fusion.place_ref
  41.3 0.9 %collective-permute-start.3 = (bf16[288,128]{1,0:T(8,128)(2,1)S(1)}, bf16[288,128]{1,0:T(8,128)(2,1)S(1)}, u32[]{:S(2)}, u32[]{:S(2)}) collective-permute-start(bf16[288,128]{1,0:T(8,128)(2,1)S(1)} %pad_maximum_fusion), channel_id=1, source_target_pairs={{0,4},{2,6},{4,0},{6,2},{8,12},{10,14},{12,8},{14,10},{16,20},{18,... | collective-permute-start | bytes 221192 | tf_op jit(solution)/shard_map/ppermute | solution.py:386
  42.2 0.0 collective-permute-done.7.refs_5_
  42.2 1.8 %collective-permute-start.2 = (bf16[288,128]{1,0:T(8,128)(2,1)S(1)}, bf16[288,128]{1,0:T(8,128)(2,1)S(1)}, u32[]{:S(2)}, u32[]{:S(2)}) collective-permute-start(bf16[288,128]{1,0:T(8,128)(2,1)S(1)} %pad_maximum_fusion), channel_id=1, source_target_pairs={{0,12},{2,14},{4,8},{6,10},{8,4},{10,6},{12,0},{14,2},{16,28},{18,... | collective-permute-start | bytes 221192 | tf_op jit(solution)/shard_map/ppermute | solution.py:386
  44.1 0.0 collective-permute-done.6.refs_4_
  44.1 0.8 %collective-permute-start.1 = (bf16[288,128]{1,0:T(8,128)(2,1)S(1)}, bf16[288,128]{1,0:T(8,128)(2,1)S(1)}, u32[]{:S(2)}, u32[]{:S(2)}) collective-permute-start(bf16[288,128]{1,0:T(8,128)(2,1)S(1)} %pad_maximum_fusion), channel_id=1, source_target_pairs={{0,2},{2,0},{4,6},{6,4},{8,10},{10,8},{12,14},{14,12},{16,18},{18,... | collective-permute-start | bytes 221192 | tf_op jit(solution)/shard_map/ppermute | solution.py:386
  44.9 0.0 collective-permute-done.5.refs_3_
  44.9 0.2 collective-permute-done.4.refs_2_
  45.1 0.0 copy-done
  45.1 3.1 %backward_first.1 = (f32[512,512]{1,0:T(8,128)S(1)}, f32[256,512]{1,0:T(8,128)S(1)}, f32[8,512]{1,0:T(8,128)S(1)}) custom-call(s32[2]{0:T(128)S(1)} %pad_add_fusion.place_ref, bf16[144,128]{1,0:T(8,128)(2,1)S(1)} %composite.1.refs_0_, bf16[144,128]{1,0:T(8,128)(2,1)S(1)} %collective-permute-done.refs_1_, ...), custom_call_target="tpu_custom_call" | custom-call | flops 4026531840 | bytes 1966080 | tf_op jit(solution)/shard_map/backward_first/pallas_call | solution.py:408
  48.2 0.0 collective-permute-done.3.refs_2_
  48.2 0.0 collective-permute-done.2.refs_1_
  48.2 0.2 collective-permute-done.1.refs_0_
  48.4 2.3 %backward_rest.1 = (bf16[1,400,512]{2,1,0:T(8,128)(2,1)S(1)}, bf16[1,400,512]{2,1,0:T(8,128)(2,1)S(1)}) custom-call(s32[2]{0:T(128)S(1)} %pad_add_fusion.place_ref, bf16[288,128]{1,0:T(8,128)(2,1)S(1)} %collective-permute-done.1.refs_0_, bf16[288,128]{1,0:T(8,128)(2,1)S(1)} %collective-permute-done.2.refs_1_, ...), custom_call_target="tpu_custom_call" | custom-call | flops 2415919104 | bytes 1179648 | tf_op jit(solution)/shard_map/backward_rest/pallas_call | solution.py:408
  50.7 0.1 collective-permute-start.8
  50.8 1.7 %collective-permute-done.8.refs_1_ = bf16[1,400,512]{2,1,0:T(8,128)(2,1)S(1)} collective-permute-done((bf16[1,400,512]{2,1,0:T(8,128)(2,1)S(1)}, bf16[1,400,512]{2,1,0:T(8,128)(2,1)S(1)}, u32[]{:S(2)}, u32[]{:S(2)}) %collective-permute-start.8) | collective-permute-done | bytes 409632 | tf_op jit(solution)/shard_map/ppermute | solution.py:456
  52.6 1.0 %settle.1 = (f32[1,128,512]{2,1,0:T(8,128)}, f32[1,256,512]{2,1,0:T(8,128)}, f32[1,256]{1,0:T(1,128)}, f32[1,1]{1,0:T(1,128)}) custom-call(bf16[1,400,512]{2,1,0:T(8,128)(2,1)S(1)} %get-tuple-element.20.refs_0_, bf16[1,400,512]{2,1,0:T(8,128)(2,1)S(1)} %collective-permute-done.8.refs_1_), custom_call_target="tpu_custom_call" | custom-call | tf_op jit(solution)/shard_map/settle/pallas_call | solution.py:459
  (7 shorter events, 0.0 us)
Async XLA Ops:
  0.6 28.7 %copy-start.1 = (bf16[512,512]{1,0:T(8,128)(2,1)S(1)}, bf16[512,512]{1,0:T(8,128)(2,1)}, u32[]{:S(2)}) copy-start(bf16[512,512]{1,0:T(8,128)(2,1)} %target_ref.1) | copy-start | bytes 1572868
  5.2 39.9 %copy-start = (bf16[1,4,512,256]{3,2,1,0:T(8,128)(2,1)S(1)}, bf16[1,4,512,256]{3,2,1,0:T(8,128)(2,1)}, u32[]{:S(2)}) copy-start(bf16[1,4,512,256]{3,2,1,0:T(8,128)(2,1)} %enc_hbm.1) | copy-start | bytes 3145732
  5.2 24.2 %all-to-all-start = ((bf16[16,136,128]{2,1,0:T(8,128)(2,1)}), bf16[16,136,128]{2,1,0:T(8,128)(2,1)S(1)}, u32[]{:S(2)}, u32[]{:S(2)}) async-start(bf16[16,136,128]{2,1,0:T(8,128)(2,1)} %get-tuple-element.15), calls=%async_computation | async-start | bytes 1114112 | tf_op jit(solution)/shard_map/all_to_all | solution.py:362
  13.6 15.7 %copy-start.4 = (s32[1,16]{1,0:T(1,128)S(1)}, s32[1,16]{1,0:T(1,128)}, u32[]{:S(2)}) copy-start(s32[1,16]{1,0:T(1,128)} %order_ref.1) | copy-start | bytes 196
  29.3 15.8 %copy-start.2 = (bf16[1,512,512]{2,1,0:T(8,128)(2,1)S(1)}, bf16[1,512,512]{2,1,0:T(8,128)(2,1)}, u32[]{:S(2)}) copy-start(bf16[1,512,512]{2,1,0:T(8,128)(2,1)} %refs_6_.1) | copy-start | bytes 1572868
  29.3 15.8 %copy-start.3 = (bf16[1,256,512]{2,1,0:T(8,128)(2,1)S(1)}, bf16[1,256,512]{2,1,0:T(8,128)(2,1)}, u32[]{:S(2)}) copy-start(bf16[1,256,512]{2,1,0:T(8,128)(2,1)} %refs_5_.1) | copy-start | bytes 786436
  29.4 15.8 %copy-start.5 = (f32[544,128]{1,0:T(8,128)S(1)}, f32[544,128]{1,0:T(8,128)}, u32[]{:S(2)}) copy-start(f32[544,128]{1,0:T(8,128)} %get-tuple-element.16) | copy-start | bytes 835588
  30.6 4.9 %collective-permute-start = (bf16[144,128]{1,0:T(8,128)(2,1)S(1)}, bf16[144,128]{1,0:T(8,128)(2,1)S(1)}, u32[]{:S(2)}, u32[]{:S(2)}) collective-permute-start(bf16[144,128]{1,0:T(8,128)(2,1)S(1)} %composite.1.refs_0_), channel_id=1, source_target_pairs={{0,16},{2,18},{4,20},{6,22},{8,24},{10,26},{12,28},{14,30},{16,0},... | collective-permute-start | bytes 110600 | tf_op jit(solution)/shard_map/ppermute | solution.py:386
  35.5 6.8 %collective-permute-start.7 = (bf16[288,128]{1,0:T(8,128)(2,1)S(1)}, bf16[288,128]{1,0:T(8,128)(2,1)S(1)}, u32[]{:S(2)}, u32[]{:S(2)}) collective-permute-start(bf16[288,128]{1,0:T(8,128)(2,1)S(1)} %pad_maximum_fusion), channel_id=1, source_target_pairs={{0,14},{2,12},{4,10},{6,8},{8,6},{10,4},{12,2},{14,0},{16,30},{18,... | collective-permute-start | bytes 221192 | tf_op jit(solution)/shard_map/ppermute | solution.py:386
  37.2 6.9 %collective-permute-start.6 = (bf16[288,128]{1,0:T(8,128)(2,1)S(1)}, bf16[288,128]{1,0:T(8,128)(2,1)S(1)}, u32[]{:S(2)}, u32[]{:S(2)}) collective-permute-start(bf16[288,128]{1,0:T(8,128)(2,1)S(1)} %pad_maximum_fusion), channel_id=1, source_target_pairs={{0,8},{2,10},{4,12},{6,14},{8,0},{10,2},{12,4},{14,6},{16,24},{18,... | collective-permute-start | bytes 221192 | tf_op jit(solution)/shard_map/ppermute | solution.py:386
  37.9 7.0 %collective-permute-start.5 = (bf16[288,128]{1,0:T(8,128)(2,1)S(1)}, bf16[288,128]{1,0:T(8,128)(2,1)S(1)}, u32[]{:S(2)}, u32[]{:S(2)}) collective-permute-start(bf16[288,128]{1,0:T(8,128)(2,1)S(1)} %pad_maximum_fusion), channel_id=1, source_target_pairs={{0,6},{2,4},{4,2},{6,0},{8,14},{10,12},{12,10},{14,8},{16,22},{18,... | collective-permute-start | bytes 221192 | tf_op jit(solution)/shard_map/ppermute | solution.py:386
  39.8 5.3 %collective-permute-start.4 = (bf16[288,128]{1,0:T(8,128)(2,1)S(1)}, bf16[288,128]{1,0:T(8,128)(2,1)S(1)}, u32[]{:S(2)}, u32[]{:S(2)}) collective-permute-start(bf16[288,128]{1,0:T(8,128)(2,1)S(1)} %pad_maximum_fusion), channel_id=1, source_target_pairs={{0,10},{2,8},{4,14},{6,12},{8,2},{10,0},{12,6},{14,4},{16,26},{18,... | collective-permute-start | bytes 221192 | tf_op jit(solution)/shard_map/ppermute | solution.py:386
  41.3 6.9 %collective-permute-start.3 = (bf16[288,128]{1,0:T(8,128)(2,1)S(1)}, bf16[288,128]{1,0:T(8,128)(2,1)S(1)}, u32[]{:S(2)}, u32[]{:S(2)}) collective-permute-start(bf16[288,128]{1,0:T(8,128)(2,1)S(1)} %pad_maximum_fusion), channel_id=1, source_target_pairs={{0,4},{2,6},{4,0},{6,2},{8,12},{10,14},{12,8},{14,10},{16,20},{18,... | collective-permute-start | bytes 221192 | tf_op jit(solution)/shard_map/ppermute | solution.py:386
  42.2 6.0 %collective-permute-start.2 = (bf16[288,128]{1,0:T(8,128)(2,1)S(1)}, bf16[288,128]{1,0:T(8,128)(2,1)S(1)}, u32[]{:S(2)}, u32[]{:S(2)}) collective-permute-start(bf16[288,128]{1,0:T(8,128)(2,1)S(1)} %pad_maximum_fusion), channel_id=1, source_target_pairs={{0,12},{2,14},{4,8},{6,10},{8,4},{10,6},{12,0},{14,2},{16,28},{18,... | collective-permute-start | bytes 221192 | tf_op jit(solution)/shard_map/ppermute | solution.py:386
  44.1 4.4 %collective-permute-start.1 = (bf16[288,128]{1,0:T(8,128)(2,1)S(1)}, bf16[288,128]{1,0:T(8,128)(2,1)S(1)}, u32[]{:S(2)}, u32[]{:S(2)}) collective-permute-start(bf16[288,128]{1,0:T(8,128)(2,1)S(1)} %pad_maximum_fusion), channel_id=1, source_target_pairs={{0,2},{2,0},{4,6},{6,4},{8,10},{10,8},{12,14},{14,12},{16,18},{18,... | collective-permute-start | bytes 221192 | tf_op jit(solution)/shard_map/ppermute | solution.py:386
  50.7 1.8 %collective-permute-start.8 = (bf16[1,400,512]{2,1,0:T(8,128)(2,1)S(1)}, bf16[1,400,512]{2,1,0:T(8,128)(2,1)S(1)}, u32[]{:S(2)}, u32[]{:S(2)}) collective-permute-start(bf16[1,400,512]{2,1,0:T(8,128)(2,1)S(1)} %get-tuple-element.21), channel_id=1, source_target_pairs={{0,1},{1,0},{2,3},{3,2},{4,5},{5,4},{6,7},{7,6},{8,9},{9,8},{10,11... | collective-permute-start | bytes 1228808 | tf_op jit(solution)/shard_map/ppermute | solution.py:456

commit v3 on v2

--- a/solution.py
+++ b/solution.py
@@ -131,14 +131,11 @@
     trans_rows = stack_rows([trans_ref[r] for r in range(regions)], LANES)
     trans = trans_rows.T[:chunk]
 
-    def tile(r, t):
-        return got_ref[r, t * chunk : (t + 1) * chunk].astype(F32)
-
-    color = [jnp.zeros((chunk, LANES), F32) for _ in range(tiles)]
-    for r in range(regions):
-        column = trans[:, r : r + 1]
-        for t in range(tiles):
-            color[t] = color[t] + column * tile(r, t)
+    def tile(t):
+        return got_ref[:, t * chunk : (t + 1) * chunk].astype(F32)
+
+    columns = jnp.stack([trans[:, r : r + 1] for r in range(regions)], axis=0)
+    color = [jnp.sum(columns * tile(t), axis=0) for t in range(tiles)]
     dcolor = []
     for t in range(tiles):
         err = color[t] - target_ref[:, t * LANES : (t + 1) * LANES].astype(F32)
@@ -146,11 +143,12 @@
     dcolor_f = [part.astype(F32) for part in dcolor]
     lanes = lax.broadcasted_iota(jnp.int32, (chunk, LANES), 1)
     terms = jnp.zeros((chunk, LANES), F32)
+    q = tile(0) * dcolor_f[0][None]
+    for t in range(1, tiles):
+        q = q + tile(t) * dcolor_f[t][None]
+    q = jnp.sum(q, axis=2, keepdims=True)
     for r in range(regions):
-        q = tile(r, 0) * dcolor_f[0]
-        for t in range(1, tiles):
-            q = q + tile(r, t) * dcolor_f[t]
-        terms = jnp.where(lanes == r, jnp.sum(q, axis=1, keepdims=True), terms)
+        terms = jnp.where(lanes == r, q[r], terms)
     terms = terms * trans
     term_rows = jnp.concatenate([terms, jnp.zeros((LANES - chunk, LANES), F32)], axis=0).T
     for r in range(regions):

time: 53.8 us -> 53.8 us (level)
  no operation moved by 1% of the time
where the time goes in v3:
time: 53.8 us; the launch traced here: 53.5 us
  waiting for transfers between devices  21.9 us (41%)
  starting transfers between devices  18.7 us (35%)
  Pallas kernels  12.1 us (22%)
  between operations  0.75 us (1%)
    all_to_all x1, waiting for transfers between devices, body(): got = lax.all_to_all(payload, 'depth', 0, 0)  15.7 us
    ppermute x8, starting transfers between devices, hop(): lax.ppermute(value, 'depth', [(o * inner + i, to(o, i)) for o in range(ou...  10.2 us
    all_to_all x1, starting transfers between devices, body(): got = lax.all_to_all(payload, 'depth', 0, 0)  8.44 us
    pallas_call x2, Pallas kernels, backward(): pl.pallas_call(functools.partial(backward_kernel, outer, flips, bool(befo...  5.41 us
    pallas_call x1, Pallas kernels, body(): pl.pallas_call(forward_kernel, in_specs=[hbm] * 5, out_specs=[hbm] * 2, o...  4.51 us
    ppermute x8, waiting for transfers between devices, hop(): lax.ppermute(value, 'depth', [(o * inner + i, to(o, i)) for o in range(ou...  4.42 us
    ppermute x1, waiting for transfers between devices, body(): parts.append(lax.ppermute(send[shift - 1:shift], 'rays', ring))  1.73 us
    pallas_call x1, Pallas kernels, body(): pl.pallas_call(composite_kernel, grid_spec=pltpu.PrefetchScalarGridSpec(n...  1.24 us
  transfers between devices with their start and end apart: 10, of which 5 were waited for; matrix products, arithmetic and copies ran while one was open for 0% of the time, Pallas kernels for 6%

profile of v3, /device:TPU:0, one launch (start us, length us, event | category | flops | bytes accessed | tf_op | source)
XLA Modules:
  0.0 53.5 jit_solution(17950520691737846953)
XLA Ops:
  0.6 4.5 %forward.1 = (bf16[16,136,128]{2,1,0:T(8,128)(2,1)}, f32[544,128]{1,0:T(8,128)}) custom-call(bf16[1,4,512,256]{3,2,1,0:T(8,128)(2,1)} %enc_hbm.1, f32[1,4,512]{2,1,0:T(4,128)} %delta_hbm.1, bf16[1,256,512]{2,1,0:T(8,128)(2,1)} %refs_5_.1, bf16[1,512,512]{2,1,0:T(8,128)(2,1)} %refs_6_.1, bf16[1,512]{1,0:T(2,128)(2,1)} %w_sig_hbm.1), custom_call_target="tpu_custom_call" | custom-call | tf_op jit(solution)/shard_map/forward/pallas_call | solution.py:336
  5.2 0.0 copy-start
  5.2 8.4 %all-to-all-start = ((bf16[16,136,128]{2,1,0:T(8,128)(2,1)}), bf16[16,136,128]{2,1,0:T(8,128)(2,1)S(1)}, u32[]{:S(2)}, u32[]{:S(2)}) async-start(bf16[16,136,128]{2,1,0:T(8,128)(2,1)} %get-tuple-element.15), calls=%async_computation | async-start | bytes 1114112 | tf_op jit(solution)/shard_map/all_to_all | solution.py:360
  13.6 0.0 copy-start.4
  13.6 15.7 %all-to-all-done.got_ref = bf16[16,136,128]{2,1,0:T(8,128)(2,1)S(1)} async-done(((bf16[16,136,128]{2,1,0:T(8,128)(2,1)}), bf16[16,136,128]{2,1,0:T(8,128)(2,1)S(1)}, u32[]{:S(2)}, u32[]{:S(2)}) %all-to-all-start) | async-done | bytes 557088 | tf_op jit(solution)/shard_map/all_to_all | solution.py:360
  29.3 0.0 copy-done.4
  29.4 0.0 copy-start.5
  29.4 1.2 %composite.1.refs_0_ = bf16[144,128]{1,0:T(8,128)(2,1)S(1)} custom-call(s32[1,16]{1,0:T(1,128)S(1)} %copy-done.4, s32[1]{0:T(128)} %bitcast.me_ref, bf16[16,136,128]{2,1,0:T(8,128)(2,1)S(1)} %all-to-all-done.got_ref, bf16[512,512]{1,0:T(8,128)(2,1)S(1)} %copy-done.1), custom_call_target="tpu_custom_call" | custom-call | tf_op jit(solution)/shard_map/composite/pallas_call | solution.py:366
  30.6 0.9 %collective-permute-start = (bf16[144,128]{1,0:T(8,128)(2,1)S(1)}, bf16[144,128]{1,0:T(8,128)(2,1)S(1)}, u32[]{:S(2)}, u32[]{:S(2)}) collective-permute-start(bf16[144,128]{1,0:T(8,128)(2,1)S(1)} %composite.1.refs_0_), channel_id=1, source_target_pairs={{0,16},{2,18},{4,20},{6,22},{8,24},{10,26},{12,28},{14,30},{16,0},... | collective-permute-start | bytes 110600 | tf_op jit(solution)/shard_map/ppermute | solution.py:384
  31.5 4.0 %collective-permute-done.refs_1_ = bf16[144,128]{1,0:T(8,128)(2,1)S(1)} collective-permute-done((bf16[144,128]{1,0:T(8,128)(2,1)S(1)}, bf16[144,128]{1,0:T(8,128)(2,1)S(1)}, u32[]{:S(2)}, u32[]{:S(2)}) %collective-permute-start) | collective-permute-done | bytes 36896 | tf_op jit(solution)/shard_map/ppermute | solution.py:384
  35.5 1.7 %collective-permute-start.7 = (bf16[288,128]{1,0:T(8,128)(2,1)S(1)}, bf16[288,128]{1,0:T(8,128)(2,1)S(1)}, u32[]{:S(2)}, u32[]{:S(2)}) collective-permute-start(bf16[288,128]{1,0:T(8,128)(2,1)S(1)} %pad_maximum_fusion), channel_id=1, source_target_pairs={{0,14},{2,12},{4,10},{6,8},{8,6},{10,4},{12,2},{14,0},{16,30},{18,... | collective-permute-start | bytes 221192 | tf_op jit(solution)/shard_map/ppermute | solution.py:384
  37.2 0.7 %collective-permute-start.6 = (bf16[288,128]{1,0:T(8,128)(2,1)S(1)}, bf16[288,128]{1,0:T(8,128)(2,1)S(1)}, u32[]{:S(2)}, u32[]{:S(2)}) collective-permute-start(bf16[288,128]{1,0:T(8,128)(2,1)S(1)} %pad_maximum_fusion), channel_id=1, source_target_pairs={{0,8},{2,10},{4,12},{6,14},{8,0},{10,2},{12,4},{14,6},{16,24},{18,... | collective-permute-start | bytes 221192 | tf_op jit(solution)/shard_map/ppermute | solution.py:384
  37.9 1.9 %collective-permute-start.5 = (bf16[288,128]{1,0:T(8,128)(2,1)S(1)}, bf16[288,128]{1,0:T(8,128)(2,1)S(1)}, u32[]{:S(2)}, u32[]{:S(2)}) collective-permute-start(bf16[288,128]{1,0:T(8,128)(2,1)S(1)} %pad_maximum_fusion), channel_id=1, source_target_pairs={{0,6},{2,4},{4,2},{6,0},{8,14},{10,12},{12,10},{14,8},{16,22},{18,... | collective-permute-start | bytes 221192 | tf_op jit(solution)/shard_map/ppermute | solution.py:384
  39.9 1.4 %collective-permute-start.4 = (bf16[288,128]{1,0:T(8,128)(2,1)S(1)}, bf16[288,128]{1,0:T(8,128)(2,1)S(1)}, u32[]{:S(2)}, u32[]{:S(2)}) collective-permute-start(bf16[288,128]{1,0:T(8,128)(2,1)S(1)} %pad_maximum_fusion), channel_id=1, source_target_pairs={{0,10},{2,8},{4,14},{6,12},{8,2},{10,0},{12,6},{14,4},{16,26},{18,... | collective-permute-start | bytes 221192 | tf_op jit(solution)/shard_map/ppermute | solution.py:384
  41.2 0.1 pad_add_fusion.place_ref
  41.3 0.9 %collective-permute-start.3 = (bf16[288,128]{1,0:T(8,128)(2,1)S(1)}, bf16[288,128]{1,0:T(8,128)(2,1)S(1)}, u32[]{:S(2)}, u32[]{:S(2)}) collective-permute-start(bf16[288,128]{1,0:T(8,128)(2,1)S(1)} %pad_maximum_fusion), channel_id=1, source_target_pairs={{0,4},{2,6},{4,0},{6,2},{8,12},{10,14},{12,8},{14,10},{16,20},{18,... | collective-permute-start | bytes 221192 | tf_op jit(solution)/shard_map/ppermute | solution.py:384
  42.3 0.0 collective-permute-done.7.refs_5_
  42.3 1.8 %collective-permute-start.2 = (bf16[288,128]{1,0:T(8,128)(2,1)S(1)}, bf16[288,128]{1,0:T(8,128)(2,1)S(1)}, u32[]{:S(2)}, u32[]{:S(2)}) collective-permute-start(bf16[288,128]{1,0:T(8,128)(2,1)S(1)} %pad_maximum_fusion), channel_id=1, source_target_pairs={{0,12},{2,14},{4,8},{6,10},{8,4},{10,6},{12,0},{14,2},{16,28},{18,... | collective-permute-start | bytes 221192 | tf_op jit(solution)/shard_map/ppermute | solution.py:384
  44.1 0.0 collective-permute-done.6.refs_4_
  44.1 0.8 %collective-permute-start.1 = (bf16[288,128]{1,0:T(8,128)(2,1)S(1)}, bf16[288,128]{1,0:T(8,128)(2,1)S(1)}, u32[]{:S(2)}, u32[]{:S(2)}) collective-permute-start(bf16[288,128]{1,0:T(8,128)(2,1)S(1)} %pad_maximum_fusion), channel_id=1, source_target_pairs={{0,2},{2,0},{4,6},{6,4},{8,10},{10,8},{12,14},{14,12},{16,18},{18,... | collective-permute-start | bytes 221192 | tf_op jit(solution)/shard_map/ppermute | solution.py:384
  44.9 0.0 collective-permute-done.5.refs_3_
  44.9 0.2 collective-permute-done.4.refs_2_
  45.1 0.0 copy-done.3
  45.1 0.0 copy-done.5
  45.1 3.1 %backward_first.1 = (f32[512,512]{1,0:T(8,128)S(1)}, f32[256,512]{1,0:T(8,128)S(1)}, f32[8,512]{1,0:T(8,128)S(1)}) custom-call(s32[2]{0:T(128)S(1)} %pad_add_fusion.place_ref, bf16[144,128]{1,0:T(8,128)(2,1)S(1)} %composite.1.refs_0_, bf16[144,128]{1,0:T(8,128)(2,1)S(1)} %collective-permute-done.refs_1_, ...), custom_call_target="tpu_custom_call" | custom-call | flops 4026531840 | bytes 1966080 | tf_op jit(solution)/shard_map/backward_first/pallas_call | solution.py:406
  48.3 0.0 collective-permute-done.3.refs_2_
  48.3 0.0 collective-permute-done.2.refs_1_
  48.3 0.2 collective-permute-done.1.refs_0_
  48.4 2.3 %backward_rest.1 = (bf16[1,400,512]{2,1,0:T(8,128)(2,1)S(1)}, bf16[1,400,512]{2,1,0:T(8,128)(2,1)S(1)}) custom-call(s32[2]{0:T(128)S(1)} %pad_add_fusion.place_ref, bf16[288,128]{1,0:T(8,128)(2,1)S(1)} %collective-permute-done.1.refs_0_, bf16[288,128]{1,0:T(8,128)(2,1)S(1)} %collective-permute-done.2.refs_1_, ...), custom_call_target="tpu_custom_call" | custom-call | flops 2415919104 | bytes 1179648 | tf_op jit(solution)/shard_map/backward_rest/pallas_call | solution.py:406
  50.8 0.1 collective-permute-start.8
  50.8 1.7 %collective-permute-done.8.refs_1_ = bf16[1,400,512]{2,1,0:T(8,128)(2,1)S(1)} collective-permute-done((bf16[1,400,512]{2,1,0:T(8,128)(2,1)S(1)}, bf16[1,400,512]{2,1,0:T(8,128)(2,1)S(1)}, u32[]{:S(2)}, u32[]{:S(2)}) %collective-permute-start.8) | collective-permute-done | bytes 409632 | tf_op jit(solution)/shard_map/ppermute | solution.py:454
  52.6 1.0 %settle.1 = (f32[1,128,512]{2,1,0:T(8,128)}, f32[1,256,512]{2,1,0:T(8,128)}, f32[1,256]{1,0:T(1,128)}, f32[1,1]{1,0:T(1,128)}) custom-call(bf16[1,400,512]{2,1,0:T(8,128)(2,1)S(1)} %get-tuple-element.20.refs_0_, bf16[1,400,512]{2,1,0:T(8,128)(2,1)S(1)} %collective-permute-done.8.refs_1_), custom_call_target="tpu_custom_call" | custom-call | tf_op jit(solution)/shard_map/settle/pallas_call | solution.py:457
  (7 shorter events, 0.0 us)
Async XLA Ops:
  0.6 28.7 %copy-start.1 = (bf16[512,512]{1,0:T(8,128)(2,1)S(1)}, bf16[512,512]{1,0:T(8,128)(2,1)}, u32[]{:S(2)}) copy-start(bf16[512,512]{1,0:T(8,128)(2,1)} %target_ref.1) | copy-start | bytes 1572868
  5.2 40.0 %copy-start = (bf16[1,4,512,256]{3,2,1,0:T(8,128)(2,1)S(1)}, bf16[1,4,512,256]{3,2,1,0:T(8,128)(2,1)}, u32[]{:S(2)}) copy-start(bf16[1,4,512,256]{3,2,1,0:T(8,128)(2,1)} %enc_hbm.1) | copy-start | bytes 3145732
  5.2 24.2 %all-to-all-start = ((bf16[16,136,128]{2,1,0:T(8,128)(2,1)}), bf16[16,136,128]{2,1,0:T(8,128)(2,1)S(1)}, u32[]{:S(2)}, u32[]{:S(2)}) async-start(bf16[16,136,128]{2,1,0:T(8,128)(2,1)} %get-tuple-element.15), calls=%async_computation | async-start | bytes 1114112 | tf_op jit(solution)/shard_map/all_to_all | solution.py:360
  13.6 15.7 %copy-start.4 = (s32[1,16]{1,0:T(1,128)S(1)}, s32[1,16]{1,0:T(1,128)}, u32[]{:S(2)}) copy-start(s32[1,16]{1,0:T(1,128)} %order_ref.1) | copy-start | bytes 196
  29.3 15.8 %copy-start.2 = (bf16[1,512,512]{2,1,0:T(8,128)(2,1)S(1)}, bf16[1,512,512]{2,1,0:T(8,128)(2,1)}, u32[]{:S(2)}) copy-start(bf16[1,512,512]{2,1,0:T(8,128)(2,1)} %refs_6_.1) | copy-start | bytes 1572868
  29.3 15.8 %copy-start.3 = (bf16[1,256,512]{2,1,0:T(8,128)(2,1)S(1)}, bf16[1,256,512]{2,1,0:T(8,128)(2,1)}, u32[]{:S(2)}) copy-start(bf16[1,256,512]{2,1,0:T(8,128)(2,1)} %refs_5_.1) | copy-start | bytes 786436
  29.4 15.8 %copy-start.5 = (f32[544,128]{1,0:T(8,128)S(1)}, f32[544,128]{1,0:T(8,128)}, u32[]{:S(2)}) copy-start(f32[544,128]{1,0:T(8,128)} %get-tuple-element.16) | copy-start | bytes 835588
  30.6 4.9 %collective-permute-start = (bf16[144,128]{1,0:T(8,128)(2,1)S(1)}, bf16[144,128]{1,0:T(8,128)(2,1)S(1)}, u32[]{:S(2)}, u32[]{:S(2)}) collective-permute-start(bf16[144,128]{1,0:T(8,128)(2,1)S(1)} %composite.1.refs_0_), channel_id=1, source_target_pairs={{0,16},{2,18},{4,20},{6,22},{8,24},{10,26},{12,28},{14,30},{16,0},... | collective-permute-start | bytes 110600 | tf_op jit(solution)/shard_map/ppermute | solution.py:384
  35.5 6.8 %collective-permute-start.7 = (bf16[288,128]{1,0:T(8,128)(2,1)S(1)}, bf16[288,128]{1,0:T(8,128)(2,1)S(1)}, u32[]{:S(2)}, u32[]{:S(2)}) collective-permute-start(bf16[288,128]{1,0:T(8,128)(2,1)S(1)} %pad_maximum_fusion), channel_id=1, source_target_pairs={{0,14},{2,12},{4,10},{6,8},{8,6},{10,4},{12,2},{14,0},{16,30},{18,... | collective-permute-start | bytes 221192 | tf_op jit(solution)/shard_map/ppermute | solution.py:384
  37.2 6.9 %collective-permute-start.6 = (bf16[288,128]{1,0:T(8,128)(2,1)S(1)}, bf16[288,128]{1,0:T(8,128)(2,1)S(1)}, u32[]{:S(2)}, u32[]{:S(2)}) collective-permute-start(bf16[288,128]{1,0:T(8,128)(2,1)S(1)} %pad_maximum_fusion), channel_id=1, source_target_pairs={{0,8},{2,10},{4,12},{6,14},{8,0},{10,2},{12,4},{14,6},{16,24},{18,... | collective-permute-start | bytes 221192 | tf_op jit(solution)/shard_map/ppermute | solution.py:384
  37.9 7.0 %collective-permute-start.5 = (bf16[288,128]{1,0:T(8,128)(2,1)S(1)}, bf16[288,128]{1,0:T(8,128)(2,1)S(1)}, u32[]{:S(2)}, u32[]{:S(2)}) collective-permute-start(bf16[288,128]{1,0:T(8,128)(2,1)S(1)} %pad_maximum_fusion), channel_id=1, source_target_pairs={{0,6},{2,4},{4,2},{6,0},{8,14},{10,12},{12,10},{14,8},{16,22},{18,... | collective-permute-start | bytes 221192 | tf_op jit(solution)/shard_map/ppermute | solution.py:384
  39.9 5.3 %collective-permute-start.4 = (bf16[288,128]{1,0:T(8,128)(2,1)S(1)}, bf16[288,128]{1,0:T(8,128)(2,1)S(1)}, u32[]{:S(2)}, u32[]{:S(2)}) collective-permute-start(bf16[288,128]{1,0:T(8,128)(2,1)S(1)} %pad_maximum_fusion), channel_id=1, source_target_pairs={{0,10},{2,8},{4,14},{6,12},{8,2},{10,0},{12,6},{14,4},{16,26},{18,... | collective-permute-start | bytes 221192 | tf_op jit(solution)/shard_map/ppermute | solution.py:384
  41.3 6.9 %collective-permute-start.3 = (bf16[288,128]{1,0:T(8,128)(2,1)S(1)}, bf16[288,128]{1,0:T(8,128)(2,1)S(1)}, u32[]{:S(2)}, u32[]{:S(2)}) collective-permute-start(bf16[288,128]{1,0:T(8,128)(2,1)S(1)} %pad_maximum_fusion), channel_id=1, source_target_pairs={{0,4},{2,6},{4,0},{6,2},{8,12},{10,14},{12,8},{14,10},{16,20},{18,... | collective-permute-start | bytes 221192 | tf_op jit(solution)/shard_map/ppermute | solution.py:384
  42.3 6.0 %collective-permute-start.2 = (bf16[288,128]{1,0:T(8,128)(2,1)S(1)}, bf16[288,128]{1,0:T(8,128)(2,1)S(1)}, u32[]{:S(2)}, u32[]{:S(2)}) collective-permute-start(bf16[288,128]{1,0:T(8,128)(2,1)S(1)} %pad_maximum_fusion), channel_id=1, source_target_pairs={{0,12},{2,14},{4,8},{6,10},{8,4},{10,6},{12,0},{14,2},{16,28},{18,... | collective-permute-start | bytes 221192 | tf_op jit(solution)/shard_map/ppermute | solution.py:384
  44.1 4.4 %collective-permute-start.1 = (bf16[288,128]{1,0:T(8,128)(2,1)S(1)}, bf16[288,128]{1,0:T(8,128)(2,1)S(1)}, u32[]{:S(2)}, u32[]{:S(2)}) collective-permute-start(bf16[288,128]{1,0:T(8,128)(2,1)S(1)} %pad_maximum_fusion), channel_id=1, source_target_pairs={{0,2},{2,0},{4,6},{6,4},{8,10},{10,8},{12,14},{14,12},{16,18},{18,... | collective-permute-start | bytes 221192 | tf_op jit(solution)/shard_map/ppermute | solution.py:384
  50.8 1.8 %collective-permute-start.8 = (bf16[1,400,512]{2,1,0:T(8,128)(2,1)S(1)}, bf16[1,400,512]{2,1,0:T(8,128)(2,1)S(1)}, u32[]{:S(2)}, u32[]{:S(2)}) collective-permute-start(bf16[1,400,512]{2,1,0:T(8,128)(2,1)S(1)} %get-tuple-element.21), channel_id=1, source_target_pairs={{0,1},{1,0},{2,3},{3,2},{4,5},{5,4},{6,7},{7,6},{8,9},{9,8},{10,11... | collective-permute-start | bytes 1228808 | tf_op jit(solution)/shard_map/ppermute | solution.py:454
